TPU v7x, 128 devices: a whole 4x4x4 slice. The times are simulated.
128 devices in a mesh: dp: 64 (over y, x_hi, z, core), tensor: 2 (over x_lo).
Axes of the slice: x: 4 (x_hi: 2, x_lo: 2; x = x_hi * 2 + x_lo), y: 4, z: 4, core: 2. Of those that a mesh axis runs over, the one named last changes fastest.
Arguments:
- tokens: bfloat16 [16384, 1536], P('dp'), may hold values from -6 to 6
- lengths: int32 [64, 4], P('dp'), may hold values from 1 to 128, 256 in all within a row
- keep_mask: int32 [16384], P('dp'), may hold values 0 or 1
- norm1_gain: bfloat16 [1536], replicated, may hold values from 0.099609375 to 1.8984375
- w_query: bfloat16 [1536, 1536], P(None, 'tensor'), may hold values from -0.15625 to 0.15625
- b_query: bfloat16 [12, 128], P('tensor'), may hold values from -3 to 3
- w_key: bfloat16 [1536, 256], P(None, 'tensor'), may hold values from -0.15625 to 0.15625
- b_key: bfloat16 [2, 128], P('tensor'), may hold values from -3 to 3
- w_value: bfloat16 [1536, 256], P(None, 'tensor'), may hold values from -0.15625 to 0.15625
- b_value: bfloat16 [2, 128], P('tensor'), may hold values from -3 to 3
- w_out: bfloat16 [1536, 1536], P('tensor'), may hold values from -0.625 to 0.625
- norm2_gain: bfloat16 [1536], replicated, may hold values from 0.099609375 to 1.8984375
- w_gate: bfloat16 [1536, 8960], P(None, 'tensor'), may hold values from -0.15625 to 0.15625
- w_up: bfloat16 [1536, 8960], P(None, 'tensor'), may hold values from -0.15625 to 0.15625
- w_down: bfloat16 [8960, 1536], P('tensor'), may hold values from -0.0625 to 0.0625
- cotangent: bfloat16 [16384, 1536], P('dp'), may hold values from -6 to 6
Outputs:
- layer_out: bfloat16 [16384, 1536], P('dp')
- d_input: bfloat16 [16384, 1536], P('dp')
- d_norm1_gain: float32 [1536], P('dp')
- d_query: float32 [1536, 1536], P('dp', 'tensor')
- d_bquery: float32 [12, 128], P('tensor')
- d_key: float32 [1536, 256], P('dp', 'tensor')
- d_bkey: float32 [2, 128], P('tensor')
- d_value: float32 [1536, 256], P('dp', 'tensor')
- d_bvalue: float32 [2, 128], P('tensor')
- d_out: float32 [1536, 1536], P('tensor', 'dp')
- d_norm2_gain: float32 [1536], P('dp')
- d_gate: float32 [1536, 8960], P('dp', 'tensor')
- d_up: float32 [1536, 8960], P('dp', 'tensor')
- d_down: float32 [8960, 1536], P('tensor', 'dp')
Inputs may be any that keep to these rules, and one draw needn't show every extreme that they name: `lengths`: each row sums to 256, and its longest document has exactly 128 tokens.
All inputs are finite; a program needn't handle non-finite values. No bound on the sum of `keep_mask` on one device may be relied on, other than what follows from the above.
Results may differ from a plain program's by a relative error of at most 0.018.
Values sent between devices are 32-bit elements; how exact they have to be, the bound alone decides.
A program may use at most 320 MiB of HBM per device.

v0:
```python
import jax
import jax.numpy as jnp
from jax import lax
from jax.sharding import PartitionSpec as P

EPS = 1e-06
ROPE_BASE = 10000.0
NEG_FILL = -1e30


def rms_scale(values):
    return lax.rsqrt(jnp.mean(values * values, axis=-1, keepdims=True) + EPS)


def rotate(values):
    half_width = values.shape[-1] // 2
    return jnp.concatenate([-values[..., half_width:], values[..., :half_width]], axis=-1)


def rotate_back(values):
    half_width = values.shape[-1] // 2
    return jnp.concatenate([values[..., half_width:], -values[..., :half_width]], axis=-1)


def tables(length_row, tok_count, width):
    positions = jnp.arange(tok_count, dtype=jnp.int32)
    doc_ends = jnp.cumsum(length_row)
    passed = (positions[:, None] >= doc_ends[None, :]).astype(jnp.int32)
    segment = jnp.sum(passed, axis=1)
    doc_place = positions - jnp.sum(passed * length_row[None, :], axis=1)
    inv_freq = ROPE_BASE ** (-jnp.arange(0, width, 2).astype(jnp.float32) / width)
    angles = doc_place.astype(jnp.float32)[:, None] * inv_freq[None, :]
    angles = jnp.concatenate([angles, angles], axis=1)
    return (segment, jnp.cos(angles), jnp.sin(angles))


def weight_grad(left, right):
    return jnp.einsum("tc,ti->ci", left, right, preferred_element_type=jnp.float32)


def input_grad(right, weight):
    return jnp.einsum("ti,ci->tc", right, weight, preferred_element_type=jnp.float32)


def norm_backward(normed_gradient, normalized_rows, row_inverse_scale, norm_gain):
    scaled_rows = normed_gradient * norm_gain
    gain_gradient = jnp.sum(normed_gradient * normalized_rows, axis=0)
    row_gradient = row_inverse_scale * (
        scaled_rows
        - normalized_rows * jnp.mean(scaled_rows * normalized_rows, axis=-1, keepdims=True)
    )
    return (gain_gradient, row_gradient)


def on_device(
    tokens,
    lengths,
    keep_mask,
    norm1_gain,
    w_query,
    b_query,
    w_key,
    b_key,
    w_value,
    b_value,
    w_out,
    norm2_gain,
    w_gate,
    w_up,
    w_down,
    cotangent,
):
    tok_count = tokens.shape[0]
    head_count, head_width = b_query.shape
    kv_local = b_key.shape[0]
    group_count = head_count // kv_local
    score_scale = head_width ** (-0.5)
    segment, cosine, sine_table = tables(lengths[0], tok_count, head_width)
    cos_h = cosine[:, None, :]
    sin_h = sine_table[:, None, :]
    positions = jnp.arange(tok_count, dtype=jnp.int32)
    allowed = (
        (segment[:, None] == segment[None, :])
        & (positions[None, :] <= positions[:, None])
        & ((keep_mask[None, :] == 1) | (positions[None, :] == positions[:, None]))
    )
    input_rows = tokens.astype(jnp.float32)
    first_norm_gain = norm1_gain.astype(jnp.float32)
    first_scale = rms_scale(input_rows)
    first_normalized = input_rows * first_scale
    first_normed = (first_normalized * first_norm_gain).astype(jnp.bfloat16)
    q_pre = jnp.dot(first_normed, w_query, preferred_element_type=jnp.float32) + b_query.reshape(
        -1
    ).astype(jnp.float32)
    k_pre = jnp.dot(first_normed, w_key, preferred_element_type=jnp.float32) + b_key.reshape(
        -1
    ).astype(jnp.float32)
    v_pre = jnp.dot(first_normed, w_value, preferred_element_type=jnp.float32) + b_value.reshape(
        -1
    ).astype(jnp.float32)
    q_three = q_pre.reshape(tok_count, head_count, head_width)
    queries = ((q_three * cos_h + rotate(q_three) * sin_h) * score_scale).astype(jnp.bfloat16)
    queries = queries.reshape(tok_count, kv_local, group_count, head_width)
    k_three = k_pre.reshape(tok_count, kv_local, head_width)
    keys = (k_three * cos_h + rotate(k_three) * sin_h).astype(jnp.bfloat16)
    v_low = v_pre.astype(jnp.bfloat16).reshape(tok_count, kv_local, head_width)
    raw_scores = jnp.einsum("tkgd,skd->kgts", queries, keys, preferred_element_type=jnp.float32)
    scores = jnp.where(allowed, raw_scores, NEG_FILL)
    row_top = jnp.max(scores, axis=-1, keepdims=True)
    exp_scores = jnp.exp(scores - row_top)
    soft_weights = exp_scores / jnp.sum(exp_scores, axis=-1, keepdims=True)
    soft_low = soft_weights.astype(jnp.bfloat16)
    attn_mix = jnp.einsum("kgts,skd->tkgd", soft_low, v_low, preferred_element_type=jnp.float32)
    attn_mix = attn_mix.reshape(tok_count, head_count * head_width).astype(jnp.bfloat16)
    attn_branch = lax.psum(jnp.dot(attn_mix, w_out, preferred_element_type=jnp.float32), "tensor")
    residual_stream = input_rows + attn_branch
    second_norm_gain = norm2_gain.astype(jnp.float32)
    second_scale = rms_scale(residual_stream)
    second_normalized = residual_stream * second_scale
    second_normed = (second_normalized * second_norm_gain).astype(jnp.bfloat16)
    gate_pre = jnp.dot(second_normed, w_gate, preferred_element_type=jnp.float32)
    up_pre = jnp.dot(second_normed, w_up, preferred_element_type=jnp.float32)
    sigmoid_gate = jax.nn.sigmoid(gate_pre)
    silu_gate = gate_pre * sigmoid_gate
    hidden_low = (silu_gate * up_pre).astype(jnp.bfloat16)
    ffn_branch = lax.psum(jnp.dot(hidden_low, w_down, preferred_element_type=jnp.float32), "tensor")
    layer_out = (residual_stream + ffn_branch).astype(jnp.bfloat16)
    d_layer = cotangent.astype(jnp.float32)
    d_down = weight_grad(hidden_low, cotangent)
    d_hidden = input_grad(cotangent, w_down)
    d_gate_low = (
        d_hidden * up_pre * sigmoid_gate * (1.0 + gate_pre * (1.0 - sigmoid_gate))
    ).astype(jnp.bfloat16)
    d_up_low = (d_hidden * silu_gate).astype(jnp.bfloat16)
    d_gate = weight_grad(second_normed, d_gate_low)
    d_up = weight_grad(second_normed, d_up_low)
    second_normed_gradient = lax.psum(
        input_grad(d_gate_low, w_gate) + input_grad(d_up_low, w_up), "tensor"
    )
    second_gain_gradient, residual_norm_gradient = norm_backward(
        second_normed_gradient, second_normalized, second_scale, second_norm_gain
    )
    d_resid = d_layer + residual_norm_gradient
    d_resid_low = d_resid.astype(jnp.bfloat16)
    d_out = weight_grad(attn_mix, d_resid_low)
    d_mix = (
        input_grad(d_resid_low, w_out)
        .astype(jnp.bfloat16)
        .reshape(tok_count, kv_local, group_count, head_width)
    )
    d_soft = jnp.einsum("tkgd,skd->kgts", d_mix, v_low, preferred_element_type=jnp.float32)
    d_scores = (
        soft_weights * (d_soft - jnp.sum(soft_weights * d_soft, axis=-1, keepdims=True))
    ).astype(jnp.bfloat16)
    d_queries = jnp.einsum("kgts,skd->tkgd", d_scores, keys, preferred_element_type=jnp.float32)
    d_keys = jnp.einsum("kgts,tkgd->skd", d_scores, queries, preferred_element_type=jnp.float32)
    d_values = jnp.einsum("kgts,tkgd->skd", soft_low, d_mix, preferred_element_type=jnp.float32)
    d_qrot = (d_queries * score_scale).reshape(tok_count, head_count, head_width)
    d_qpre = (
        (d_qrot * cos_h + rotate_back(d_qrot * sin_h))
        .reshape(tok_count, head_count * head_width)
        .astype(jnp.bfloat16)
    )
    d_kpre = (
        (d_keys * cos_h + rotate_back(d_keys * sin_h))
        .reshape(tok_count, kv_local * head_width)
        .astype(jnp.bfloat16)
    )
    d_vpre = d_values.reshape(tok_count, kv_local * head_width).astype(jnp.bfloat16)
    d_query = weight_grad(first_normed, d_qpre)
    d_key = weight_grad(first_normed, d_kpre)
    d_value = weight_grad(first_normed, d_vpre)
    local_bquery = jnp.sum(d_qpre.astype(jnp.float32), axis=0).reshape(head_count, head_width)
    local_bkey = jnp.sum(d_kpre.astype(jnp.float32), axis=0).reshape(kv_local, head_width)
    local_bvalue = jnp.sum(d_vpre.astype(jnp.float32), axis=0).reshape(kv_local, head_width)
    d_bquery, d_bkey, d_bvalue = lax.psum((local_bquery, local_bkey, local_bvalue), "dp")
    d_none_part = (
        input_grad(d_qpre, w_query) + input_grad(d_kpre, w_key) + input_grad(d_vpre, w_value)
    )
    first_normed_gradient = lax.psum(d_none_part, "tensor")
    first_gain_gradient, input_norm_gradient = norm_backward(
        first_normed_gradient, first_normalized, first_scale, first_norm_gain
    )
    d_input = (d_resid + input_norm_gradient).astype(jnp.bfloat16)
    first_sum, query_sum, key_sum, value_sum, out_sum, second_sum, gate_sum, up_sum, down_sum = (
        lax.psum_scatter(first_gain_gradient, "dp", scatter_dimension=0, tiled=True),
        lax.psum_scatter(d_query, "dp", scatter_dimension=0, tiled=True),
        lax.psum_scatter(d_key, "dp", scatter_dimension=0, tiled=True),
        lax.psum_scatter(d_value, "dp", scatter_dimension=0, tiled=True),
        lax.psum_scatter(d_out, "dp", scatter_dimension=1, tiled=True),
        lax.psum_scatter(second_gain_gradient, "dp", scatter_dimension=0, tiled=True),
        lax.psum_scatter(d_gate, "dp", scatter_dimension=0, tiled=True),
        lax.psum_scatter(d_up, "dp", scatter_dimension=0, tiled=True),
        lax.psum_scatter(d_down, "dp", scatter_dimension=1, tiled=True),
    )
    return (
        layer_out,
        d_input,
        first_sum,
        query_sum,
        d_bquery,
        key_sum,
        d_bkey,
        value_sum,
        d_bvalue,
        out_sum,
        second_sum,
        gate_sum,
        up_sum,
        down_sum,
    )


def solution(mesh):
    placed = (
        P("dp", None),
        P("dp", None),
        P("dp"),
        P(),
        P(None, "tensor"),
        P("tensor", None),
        P(None, "tensor"),
        P("tensor", None),
        P(None, "tensor"),
        P("tensor", None),
        P("tensor", None),
        P(),
        P(None, "tensor"),
        P(None, "tensor"),
        P("tensor", None),
        P("dp", None),
    )
    return jax.shard_map(
        on_device,
        mesh=mesh,
        in_specs=placed,
        out_specs=(
            P("dp", None),
            P("dp", None),
            P("dp"),
            P("dp", "tensor"),
            P("tensor", None),
            P("dp", "tensor"),
            P("tensor", None),
            P("dp", "tensor"),
            P("tensor", None),
            P("tensor", "dp"),
            P("dp"),
            P("dp", "tensor"),
            P("dp", "tensor"),
            P("tensor", "dp"),
        ),
        check_vma=False,
    )
```

profile of v0, /device:TPU:1, one launch (start us, length us, event | category | flops | bytes accessed | tf_op | source)
XLA Modules:
  0.0 1706.8 jit_solution(15814349287167790755)
XLA Ops:
  7.3 1.4 broadcast_compare_fusion
  9.3 1.2 bitcast_convert_fusion.2
  10.5 1.4 fusion.12
  14.8 1.7 convolution_add_fusion.4
  17.9 3.4 convolution_add_fusion.3
  21.2 2.3 copy.73
  23.6 1.5 fusion.40
  26.1 2.3 copy.72
  28.4 1.2 slice_negate_fusion.1
  30.5 2.3 copy.74
  32.8 2.5 multiply_convert_fusion.5
  35.3 1.9 copy.75
  38.1 1.4 fusion.21
  41.9 1.9 fusion.70
  44.8 60.5 %all-reduce.13.cloned.1.call-done = f32[256,1536]{1,0:T(8,128)} async-done(((f32[256,1536]{1,0:T(8,128)}), f32[256,1536]{1,0:T(8,128)}) %all-reduce.13.cloned.1.call-update) | async-done | bytes 1572880 | tf_op jit(solution)/shard_map/psum | solution.py:115
  105.3 1.7 multiply_reduce_fusion.2
  108.4 10.7 fusion.72
  119.1 10.4 fusion.71
  129.5 19.9 %multiply_convert_fusion = (bf16[256,4480]{1,0:T(8,128)(2,1)}, bf16[256,4480]{1,0:T(8,128)(2,1)S(1)}, bf16[256,4480]{1,0:T(8,128)(2,1)}) fusion(f32[256,4480]{1,0:T(8,128)} %fusion.71, f32[256,4480]{1,0:T(8,128)} %fusion.72, bf16[256,1536]{1,0:T(8,128)(2,1)S(1)} %copy-done.15, bf16[4480,1536]{1,0:T(8,128)(2,1)} %param.30), kind=kOutput, calls=%fused_computation | convolution fusion | flops 3540418560 | bytes 30605312 | tf_op jit(solution)/shard_map/ti,ci->tc/dot_general | solution.py:42
  149.4 7.9 fusion.74
  157.4 8.5 convolution_add_fusion.2
  166.2 10.6 fusion.73
  176.7 48.3 %all-reduce.15.cloned.1.call-done = f32[256,1536]{1,0:T(8,128)} async-done(((f32[256,1536]{1,0:T(8,128)}), f32[256,1536]{1,0:T(8,128)}) %all-reduce.15.cloned.1.call-update) | async-done | bytes 1572880 | tf_op jit(solution)/shard_map/psum | solution.py:137
  225.1 3.1 multiply_reduce_fusion
  228.2 1.6 multiply_add_fusion
  229.8 1.3 copy-done.5
  231.1 1.6 convolution_convert_fusion
  232.6 1.2 copy.80
  233.8 2.6 convert_reduce_fusion.1
  239.8 1.4 copy-done.18
  243.5 1.5 convolution_add_fusion
  245.9 1.4 fusion.58
  247.4 1.4 fusion.51
  248.9 2.9 fusion.30
  251.9 3.1 fusion.61
  255.3 1.8 copy-done.14
  257.1 12.4 fusion.78
  270.7 12.8 fusion.77
  283.6 12.9 fusion.76
  298.5 40.3 %all-reduce.17.cloned.1.call-done = (f32[256,1536]{1,0:T(8,128)}, f32[256,1536]{1,0:T(8,128)}) async-done(((f32[256,1536]{1,0:T(8,128)}, f32[256,1536]{1,0:T(8,128)}), (f32[256,1536]{1,0:T(8,128)}, f32[256,1536]{1,0:T(8,128)})) %all-reduce.17.cloned.1.call-update) | async-done | bytes 3145744 | tf_op jit(solution)/shard_map/psum | solution.py:126
  338.8 1.9 fusion.11
  340.8 322.4 %all-reduce.7 = (f32[1536]{0:T(1024)S(1)}, f32[6,128]{1,0:T(8,128)}, f32[1,128]{1,0:T(1,128)}, f32[1,128]{1,0:T(1,128)}, f32[1536]{0:T(1024)S(1)}) all-reduce(f32[1536]{0:T(1024)S(1)} %get-tuple-element.16, f32[6,128]{1,0:T(8,128)S(1)} %get-tuple-element.34, ...), channel_id=2, replica_groups=mesh['dp'=64,'tensor'=2] {'dp'}, use_global_device_ids=true, to_apply=%region_15.16.clone | all-reduce | flops 4096 | bytes 32768
  664.3 4.6 fusion.10
  669.0 123.1 %reduce-scatter.20.cloned.1.call-done = f32[768,24]{0,1:T(8,128)} async-done(((f32[768,1536]{0,1:T(8,128)}), f32[768,24]{0,1:T(8,128)}) %reduce-scatter.20.cloned.1.call-update) | async-done | bytes 73744 | tf_op jit(solution)/shard_map/reduce_scatter | solution.py:190
  792.1 159.5 %reduce-scatter.18.cloned.1.call-done = f32[24,768]{1,0:T(8,128)} async-done(((f32[1536,768]{1,0:T(8,128)}), f32[24,768]{1,0:T(8,128)}) %reduce-scatter.18.cloned.1.call-update) | async-done | bytes 73744 | tf_op jit(solution)/shard_map/reduce_scatter | solution.py:187
  951.6 249.9 %reduce-scatter.30.cloned.1.call-done = f32[4480,24]{0,1:T(8,128)} async-done(((f32[4480,1536]{0,1:T(8,128)}), f32[4480,24]{0,1:T(8,128)}) %reduce-scatter.30.cloned.1.call-update) | async-done | bytes 430096
  1201.5 249.4 %reduce-scatter.28.cloned.1.call-done = f32[24,4480]{1,0:T(8,128)} async-done(((f32[1536,4480]{1,0:T(8,128)}), f32[24,4480]{1,0:T(8,128)}) %reduce-scatter.28.cloned.1.call-update) | async-done | bytes 430096
  1450.9 249.1 %reduce-scatter.26.cloned.1.call-done = f32[24,4480]{1,0:T(8,128)} async-done(((f32[1536,4480]{1,0:T(8,128)}), f32[24,4480]{1,0:T(8,128)}) %reduce-scatter.26.cloned.1.call-update) | async-done | bytes 430096
  (134 shorter events, 23.4 us)
Async XLA Ops:
  7.2 34.8 %copy-start = (bf16[768,1536]{1,0:T(8,128)(2,1)S(1)}, bf16[768,1536]{1,0:T(8,128)(2,1)}, u32[]{:S(2)}) copy-start(bf16[768,1536]{1,0:T(8,128)(2,1)} %param.26) | copy-start | bytes 7077892
  7.2 10.7 copy-start.2
  7.2 98.1 %all-reduce.13.cloned.1.call-start = ((), (), s32[]{:S(2)}) async-start(), calls=%async_computation.7 | async-start | bytes 3145728 | tf_op jit(solution)/shard_map/psum | solution.py:115
  11.9 26.3 %copy-start.29 = (f32[256]{0:T(256)}, f32[256]{0:T(256)S(1)}, u32[]{:S(2)}) copy-start(f32[256]{0:T(256)S(1)} %add_rsqrt_fusion.1) | copy-start | bytes 3076
  37.3 2.3 copy-start.21
  39.5 0.7 copy-start.38
  40.0 1.2 copy-start.7
  40.0 1.2 copy-start.27
  40.2 1.0 copy-start.31
  41.2 0.7 copy-start.16
  43.9 181.2 %all-reduce.15.cloned.1.call-start = ((), (), s32[]{:S(2)}) async-start(), calls=%async_computation.8 | async-start | bytes 3145728 | tf_op jit(solution)/shard_map/psum | solution.py:137
  107.0 1.2 copy-start.3
  107.0 1.1 copy-start.34
  108.4 10.7 copy-start.11
  119.1 10.4 copy-start.15
  149.4 7.9 copy-start.19
  149.4 8.0 copy-start.20
  165.9 172.9 %all-reduce.17.cloned.1.call-start = ((), (), s32[]{:S(2)}) async-start(), calls=%async_computation.16 | async-start | bytes 6291456 | tf_op jit(solution)/shard_map/psum | solution.py:126
  225.1 3.1 copy-start.4
  225.1 3.1 copy-start.13
  225.1 3.1 copy-start.35
  229.8 1.3 copy-start.5
  231.1 2.7 copy-start.28
  233.8 2.6 copy-start.8
  233.8 2.6 copy-start.32
  233.8 2.6 copy-start.39
  236.4 6.5 copy-start.25
  237.3 1.1 copy-start.9
  237.3 1.4 copy-start.10
  239.5 1.7 copy-start.18
  241.2 1.3 copy-start.23
  242.5 1.0 copy-start.24
  245.1 0.8 copy-start.26
  245.1 0.8 copy-start.30
  245.1 423.8 %reduce-scatter.24.cloned.1.call-start = ((), (), s32[]{:S(2)}) async-start(), calls=%async_computation.12 | async-start | bytes 798720
  247.4 1.6 copy-start.6
  247.4 1.6 copy-start.17
  247.4 421.6 %reduce-scatter.22.cloned.1.call-start = ((), (), s32[]{:S(2)}) async-start(), calls=%async_computation.11 | async-start | bytes 798720
  248.9 543.2 %reduce-scatter.20.cloned.1.call-start = ((), (), s32[]{:S(2)}) async-start(), calls=%async_computation.10 | async-start | bytes 4792320 | tf_op jit(solution)/shard_map/reduce_scatter | solution.py:190
  251.9 699.7 %reduce-scatter.18.cloned.1.call-start = ((), (), s32[]{:S(2)}) async-start(), calls=%async_computation.9 | async-start | bytes 4792320 | tf_op jit(solution)/shard_map/reduce_scatter | solution.py:187
  255.0 2.2 copy-start.14
  255.0 946.5 %reduce-scatter.30.cloned.1.call-start = ((), (), s32[]{:S(2)}) async-start(), calls=%async_computation.15 | async-start | bytes 27955200
  269.6 1.1 copy-start.12
  269.6 1181.3 %reduce-scatter.28.cloned.1.call-start = ((), (), s32[]{:S(2)}) async-start(), calls=%async_computation.14 | async-start | bytes 27955200
  283.6 1416.4 %reduce-scatter.26.cloned.1.call-start = ((), (), s32[]{:S(2)}) async-start(), calls=%async_computation.13 | async-start | bytes 27955200
  296.6 44.1 %copy-start.33 = (f32[1536]{0:T(1024)S(1)}, f32[1536]{0:T(1024)}, u32[]{:S(2)}) copy-start(f32[1536]{0:T(1024)} %get-tuple-element.14) | copy-start | bytes 18436
  296.6 44.1 %copy-start.36 = (f32[128]{0:T(128)S(1)}, f32[128]{0:T(128)}, u32[]{:S(2)}) copy-start(f32[128]{0:T(128)} %get-tuple-element.57) | copy-start | bytes 1540
  664.3 1035.7 %copy-start.1 = (bf16[768,1536]{1,0:T(8,128)(2,1)S(1)}, bf16[768,1536]{1,0:T(8,128)(2,1)}, u32[]{:S(2)}) copy-start(bf16[768,1536]{1,0:T(8,128)(2,1)} %param.26) | copy-start | bytes 7077892
  (2 other events, 1.3 us)
Sparse Core Ops, SparseCore 0:
  44.0 61.2 all-reduce.12
  166.0 59.0 all-reduce.14
  245.2 93.5 all-reduce.16
  345.1 141.9 reduce-scatter.23
  492.6 140.1 reduce-scatter.21
  639.5 152.5 reduce-scatter.19
  798.9 152.5 reduce-scatter.17
  959.4 242.0 reduce-scatter.29
  1209.4 241.4 reduce-scatter.27
  1458.6 241.3 reduce-scatter.25
where the time goes:
time: 1710 us
  waiting for transfers between devices  1180 us (69%)
  blocking collectives  322 us (19%)
  matrix products  133 us (8%)
  other arithmetic  30.7 us (2%)
  local copies, waits for them, and re-layouts  24.4 us (1%)
    unnamed x15, waiting for transfers between devices  749 us
    unnamed x1, blocking collectives  322 us
    reduce_scatter x1, waiting for transfers between devices, on_device(): lax.psum_scatter(d_query, 'dp', scatter_dimension=0, tiled=True)  160 us
    reduce_scatter x1, waiting for transfers between devices, on_device(): lax.psum_scatter(d_out, 'dp', scatter_dimension=1, tiled=True)  123 us
    psum x1, waiting for transfers between devices, on_device(): lax.psum(jnp.dot(attn_mix, w_out, preferred_element_type=jnp.float32), 't...  60.5 us
    psum x1, waiting for transfers between devices, on_device(): lax.psum(input_grad(d_gate_low, w_gate) + input_grad(d_up_low, w_up), 'te...  48.3 us
    dot_general x7, matrix products, weight_grad(): jnp.einsum('tc,ti->ci', left, right, preferred_element_type=jnp.float32)  47 us
    dot_general x7, matrix products, input_grad(): jnp.einsum('ti,ci->tc', right, weight, preferred_element_type=jnp.float32)  40.6 us
  transfers between devices with their start and end apart: 10, of which 8 were waited for; matrix products, arithmetic and copies ran while one was open for 4% of the time, Pallas kernels for 0%

commit v1 on v0

v1 whole, which is shorter than its diff:
```python
import functools

import jax
import jax.numpy as jnp
from jax import lax
from jax.experimental import pallas as pl
from jax.experimental.pallas import tpu as pltpu
from jax.sharding import PartitionSpec as P

EPS = 1e-06
ROPE_BASE = 10000.0
NEG_FILL = -1e30
MESH = pl.DeviceIdType.MESH
BF = jnp.bfloat16
F32 = jnp.float32
VM = pltpu.VMEM

D = 1536
TOK = 256
HALF = 128
HEADS = 6
WIDTH = 128
QW = HEADS * WIDTH
FFL = 4480
FFW = 1152
OFFS = (0, 1152, 2304, 3328)

UW = 256
NU = 17
GATE_UNITS = 9
G_SLOTS = 8
R_SLOTS = 3
N_TICK = NU + 6


def coords():
    dp = lax.axis_index("dp")
    t = lax.axis_index("tensor")
    return dp // 16, lax.rem(dp // 8, 2), lax.rem(dp // 2, 4), lax.rem(dp, 2), t


def device(y, xh, z, c, t):
    return (((y * 2 + xh) * 4 + z) * 2 + c, t)


def device_x(y, x, z, c):
    return device(y, x // 2, z, c, lax.rem(x, 2))


def remote(src, dst, send, recv, to):
    return pltpu.make_async_remote_copy(
        src_ref=src, dst_ref=dst, send_sem=send, recv_sem=recv, device_id=to, device_id_type=MESH
    )


def greet(devices):
    barrier = pltpu.get_barrier_semaphore()
    for to in devices:
        pl.semaphore_signal(barrier, inc=1, device_id=to, device_id_type=MESH)
    pl.semaphore_wait(barrier, len(devices))


def dot(left, right):
    return jnp.dot(left, right, preferred_element_type=F32)


def dot_nt(left, right):
    return lax.dot_general(left, right, (((1,), (1,)), ((), ())), preferred_element_type=F32)


def dot_tn(left, right):
    return lax.dot_general(left, right, (((0,), (0,)), ((), ())), preferred_element_type=F32)


def rope(v, cosine, sine):
    return v * cosine + pltpu.roll(v, WIDTH // 2, 1) * sine


def rope_back(w, cosine, sine):
    return w * cosine + pltpu.roll(w * sine, WIDTH // 2, 1)


def mean_last(v):
    return jnp.mean(v, axis=-1, keepdims=True)


def front_kernel(
    tokens, cot, lengths, keep, inv_freq, g1, wq, bq, wk, bk, wv, bv, wo, g2,
    q_o, k_o, v_o, mask_o, cos_o, sin_o, h1_o, n2_o, n2t_o, dy_o, dyt_o, la_o, o2_o,
    n2f, dyf, n1f, n1r, of, orr, part, prec, ss, rs,
):
    y, xh, z, c, t = coords()
    x = 2 * xh + t
    right = device_x(y, lax.rem(x + 1, 4), z, c)
    left = device_x(y, lax.rem(x + 3, 4), z, c)
    core = device(y, xh, z, 1 - c, t)
    mate = device(y, xh, z, c, 1 - t)
    cross = device_x(y, 3 - x, z, c)
    greet((right, left, core))
    me = 2 * xh + c
    mine = pl.ds(pl.multiple_of(t * HALF, HALF), HALF)
    other = pl.ds(pl.multiple_of((1 - t) * HALF, HALF), HALF)

    def send(i, src, dst, to):
        copy = remote(src, dst, ss.at[i], rs.at[i], to)
        copy.start()
        return copy

    dyf[me] = cot[...].astype(F32)
    dy_cross = send(0, dyf.at[me, mine], dyf.at[me, mine], cross)
    dy_core = send(1, dyf.at[me], dyf.at[me], core)

    rows = lax.broadcasted_iota(jnp.int32, (TOK, TOK), 0)
    cols = lax.broadcasted_iota(jnp.int32, (TOK, TOK), 1)
    place = lax.broadcasted_iota(jnp.int32, (TOK, WIDTH), 0)
    row_id = place
    seg_r = jnp.zeros((TOK, TOK), jnp.int32)
    seg_c = jnp.zeros((TOK, TOK), jnp.int32)
    end = jnp.int32(0)
    for i in range(4):
        span = lengths[0, i]
        end = end + span
        seg_r = seg_r + (rows >= end).astype(jnp.int32)
        seg_c = seg_c + (cols >= end).astype(jnp.int32)
        place = place - jnp.where(row_id >= end, span, 0)
    allowed = (seg_r == seg_c) & (cols <= rows) & ((keep[...] == 1) | (cols == rows))
    mask_o[...] = allowed.astype(F32)
    angle = place.astype(F32) * inv_freq[...]
    lane = lax.broadcasted_iota(jnp.int32, (TOK, WIDTH), 1)
    cosine = jnp.cos(angle)
    sine = jnp.sin(angle) * jnp.where(lane < WIDTH // 2, -1.0, 1.0)
    cos_o[...] = cosine
    sin_o[...] = sine

    xf = tokens[...].astype(F32)
    r1 = lax.rsqrt(mean_last(xf * xf) + EPS)
    n1 = (xf * r1 * g1[...]).astype(BF)
    n1f[...] = n1.astype(F32)
    n1_core = send(2, n1f, n1r, core)
    kp = dot(n1, wk[...]) + bk[...]
    k_o[...] = rope(kp, cosine, sine).astype(BF)
    v_o[...] = (dot(n1, wv[...]) + bv[...]).astype(BF)
    for h in range(HEADS):
        at = slice(h * WIDTH, (h + 1) * WIDTH)
        qp = dot(n1, wq[:, at]) + bq[:, at]
        q_o[:, at] = (rope(qp, cosine, sine) * WIDTH**-0.5).astype(BF)

    def head(h, _):
        at = pl.ds(pl.multiple_of(h * WIDTH, WIDTH), WIDTH)
        s = jnp.where(mask_o[...] > 0.5, dot_nt(q_o[:, at], k_o[...]), NEG_FILL)
        e = jnp.exp(s - jnp.max(s, axis=-1, keepdims=True))
        soft = (e / jnp.sum(e, axis=-1, keepdims=True)).astype(BF)
        o = dot(soft, v_o[...]).astype(BF)
        o2_o[:TOK, at] = o
        of[:, at] = o.astype(F32)
        return 0

    lax.fori_loop(0, HEADS, head, 0)
    part[0] = dot(o2_o[other, :], wo[...])
    half = send(3, part.at[0], prec, mate)
    o_core = send(4, of, orr, core)
    part[1] = dot(o2_o[mine, :], wo[...])

    dy_cross.wait_recv()
    far = 2 * (1 - xh) + c
    dy_pass = send(5, dyf.at[far, other], dyf.at[far, other], mate)

    half.wait_recv()
    h1 = tokens[mine, :].astype(F32) + part[1] + prec[...]
    h1_o[...] = h1
    r2 = lax.rsqrt(mean_last(h1 * h1) + EPS)
    n2f[me, mine] = (h1 * r2 * g2[...]).astype(BF).astype(F32)

    own = n2f.at[me, mine]
    to_right = send(6, own, own, right)
    to_left = send(7, own, own, left)
    to_core = send(8, own, own, core)

    la_o[:, :TOK] = n1.T
    n1_core.wait_recv()
    la_o[:, TOK:] = n1r[...].astype(BF).T
    o_core.wait_recv()
    o2_o[TOK:, :] = orr[...].astype(BF)

    def dy_block(b):
        low = dyf[b].astype(BF)
        at = pl.ds(pl.multiple_of(b * TOK, TOK), TOK)
        dy_o[at, :] = low
        dyt_o[:, at] = low.T

    dy_block(me)
    dy_core.wait_recv()
    dy_block(2 * xh + 1 - c)

    def slot(xx):
        return n2f.at[2 * (xx // 2) + c, pl.ds(pl.multiple_of(lax.rem(xx, 2) * HALF, HALF), HALF)]

    def lower(ref):
        return ref.at[pl.ds(0, HALF // 2)]

    def upper(ref):
        return ref.at[pl.ds(HALF // 2, HALF // 2)]

    from_left = slot(lax.rem(x + 3, 4))
    from_right = slot(lax.rem(x + 1, 4))
    to_right.wait_recv()
    pass_right = send(9, lower(from_left), lower(from_left), right)
    core_left = send(10, from_left, from_left, core)
    to_left.wait_recv()
    pass_left = send(11, upper(from_right), upper(from_right), left)
    core_right = send(12, from_right, from_right, core)

    dy_pass.wait_recv()
    dy_far = send(13, dyf.at[far], dyf.at[far], core)
    dy_block(far)

    pass_right.wait_recv()
    pass_left.wait_recv()
    across = slot(lax.rem(x + 2, 4))
    core_across = send(14, across, across, core)
    dy_far.wait_recv()
    dy_block(2 * (1 - xh) + 1 - c)

    def n2_block(b):
        low = n2f[b].astype(BF)
        at = pl.ds(pl.multiple_of(b * TOK, TOK), TOK)
        n2_o[at, :] = low
        n2t_o[:, at] = low.T

    n2_block(me)
    n2_block(far)
    to_core.wait_recv()
    core_left.wait_recv()
    core_right.wait_recv()
    core_across.wait_recv()
    n2_block(2 * xh + 1 - c)
    n2_block(2 * (1 - xh) + 1 - c)
    for copy in (
        dy_cross, dy_core, n1_core, half, o_core, dy_pass, to_right, to_left, to_core,
        pass_right, core_left, pass_left, core_right, dy_far, core_across,
    ):
        copy.wait_send()


def front(*args):
    shape = jax.ShapeDtypeStruct
    whole = pl.BlockSpec(memory_space=VM)
    scalars = pl.BlockSpec(memory_space=pltpu.SMEM)
    return pl.pallas_call(
        front_kernel,
        name="front",
        out_shape=(
            shape((TOK, QW), BF), shape((TOK, WIDTH), BF), shape((TOK, WIDTH), BF),
            shape((TOK, TOK), F32), shape((TOK, WIDTH), F32), shape((TOK, WIDTH), F32),
            shape((HALF, D), F32),
            shape((4 * TOK, D), BF), shape((D, 4 * TOK), BF),
            shape((4 * TOK, D), BF), shape((D, 4 * TOK), BF),
            shape((D, 2 * TOK), BF), shape((2 * TOK, QW), BF),
        ),
        in_specs=[whole, whole, scalars] + [whole] * 11,
        out_specs=(whole,) * 13,
        scratch_shapes=[
            VM((4, TOK, D), F32), VM((4, TOK, D), F32),
            VM((TOK, D), F32), VM((TOK, D), F32),
            VM((TOK, QW), F32), VM((TOK, QW), F32),
            VM((2, HALF, D), F32), VM((HALF, D), F32),
            pltpu.SemaphoreType.DMA((15,)), pltpu.SemaphoreType.DMA((15,)),
        ],
        compiler_params=pltpu.CompilerParams(
            collective_id=1, has_side_effects=True, vmem_limit_bytes=60 * 2**20
        ),
    )(*args)


def ffn_kernel(n2, dy, wg_hbm, wu_hbm, wd_hbm, dgu_o, a_o, dn2_o, out_o, wg, wu, wd, sem):
    _, xh, _, c, _ = coords()
    me = 2 * xh + c
    start = pl.multiple_of((me * 9 - me // 3) * 128, 128)
    at = pl.ds(start, FFW)
    copies = [
        pltpu.make_async_copy(wg_hbm.at[:, at], wg, sem.at[0]),
        pltpu.make_async_copy(wu_hbm.at[:, at], wu, sem.at[1]),
        pltpu.make_async_copy(wd_hbm.at[at, :], wd, sem.at[2]),
    ]
    for copy in copies:
        copy.start()
    lane = lax.broadcasted_iota(jnp.int32, (1, FFW), 1)
    live = jnp.where((lane < 128) & (me == 3), 0.0, 1.0)
    for copy in copies:
        copy.wait()

    def block(i, _):
        rows = pl.ds(pl.multiple_of(i * TOK, TOK), TOK)
        g = dot(n2[rows, :], wg[...])
        u = dot(n2[rows, :], wu[...])
        sg = live / (1.0 + jnp.exp(-g))
        silu = g * sg
        a = (silu * u).astype(BF)
        a_o[rows, :] = a
        da = dot_nt(dy[rows, :], wd[...])
        dg = (da * u * sg * (1.0 + g * (1.0 - sg))).astype(BF)
        du = (da * silu).astype(BF)
        dgu_o[rows, :FFW] = dg
        dgu_o[rows, FFW:] = du
        dn2_o[rows, :] = dot_nt(dg, wg[...]) + dot_nt(du, wu[...])
        out_o[rows, :] = dot(a, wd[...])
        return 0

    lax.fori_loop(0, 4, block, 0)


def ffn(*args):
    shape = jax.ShapeDtypeStruct
    whole = pl.BlockSpec(memory_space=VM)
    hbm = pl.BlockSpec(memory_space=pl.ANY)
    return pl.pallas_call(
        ffn_kernel,
        name="ffn",
        out_shape=(
            shape((4 * TOK, 2 * FFW), BF), shape((4 * TOK, FFW), BF),
            shape((4 * TOK, D), F32), shape((4 * TOK, D), F32),
        ),
        in_specs=[whole, whole, hbm, hbm, hbm],
        out_specs=(whole,) * 4,
        scratch_shapes=[
            VM((D, FFW), BF), VM((D, FFW), BF), VM((FFW, D), BF), pltpu.SemaphoreType.DMA((3,)),
        ],
        compiler_params=pltpu.CompilerParams(vmem_limit_bytes=60 * 2**20),
    )(*args)


def back_kernel(
    n2t, dyt, dgu_h, a_h, dn2_h, out_h, la, o2, tokens, cot, h1, q, k, v, mask, cos, sin,
    g1, g2, wq, wk, wv, wo,
    gate_o, up_o, down_o, dq_o, dk_o, dv_o, dout_o, lout_o, din_o, small_o,
    F, G, R1, R2, RB, C, L, S1, S2, dhf, dhr, dh, lb, do, dqf, xqr, rq, dkvf, xkvr, rkv,
    dn1, dn1r, dir, lof, small, sb,
    ss, rs, fss, frs, credit, xss, xrs, free, lsem, bsem, sss, srs,
):
    y, xh, z, c, t = coords()
    x = 2 * xh + t
    me = 2 * xh + c
    by_y = tuple(device(lax.rem(y + i, 4), xh, z, c, t) for i in (1, 2, 3))
    by_z = tuple(device(y, xh, lax.rem(z + i, 4), c, t) for i in (1, 2, 3))
    ring = {"y": (by_y[0], by_y[2]), "z": (by_z[0], by_z[2])}
    right = device_x(y, lax.rem(x + 1, 4), z, c)
    left = device_x(y, lax.rem(x + 3, 4), z, c)
    core = device(y, xh, z, 1 - c, t)
    mate = device(y, xh, z, c, 1 - t)
    over = device(y, 1 - xh, z, c, t)
    over_core = device(y, 1 - xh, z, 1 - c, t)
    peers = (None, core, over, over_core)
    greet(by_y + by_z + (right, left, core, over, over_core))
    mine = pl.ds(pl.multiple_of(t * HALF, HALF), HALF)
    other = pl.ds(pl.multiple_of((1 - t) * HALF, HALF), HALF)

    def way(j, stage):
        axis = "y" if (j // 2 == 0) == (stage == 0) else "z"
        return axis, (y if axis == "y" else z), (1 if j % 2 == 0 else -1)

    def chunk(g, j, stage, i):
        jx, jc = j // 2, j % 2
        if stage == 0:
            return G.at[g, i, 0, :, jc] if jx == 0 else G.at[g, :, 1, i, jc]
        return G.at[g, y, 0, i, jc] if jx == 0 else G.at[g, i, 1, z, jc]

    def step_copy(u, s, j):
        stage, n = (0, s) if s <= 3 else (1, s - 3)
        axis, p, d = way(j, stage)
        g, r = lax.rem(u, G_SLOTS), lax.rem(u, R_SLOTS)
        return remote(
            chunk(g, j, stage, lax.rem(p - d * n + 8, 4)),
            (R2 if stage else R1).at[r, n - 1, j],
            ss.at[r, s - 1, j],
            rs.at[r, s - 1, j],
            ring[axis][0 if d == 1 else 1],
        )

    def last_copy(u, n):
        px = 1 - xh if n & 2 else xh
        pc = 1 - c if n & 1 else c
        return remote(
            G.at[lax.rem(u, G_SLOTS), y, px, z, pc],
            F.at[me, u],
            fss.at[u, n - 1],
            frs.at[u, n - 1],
            peers[n],
        )

    def load(u, act):
        r = lax.rem(u, 2)

        @pl.when(u < 9)
        def _():
            at = pl.ds(pl.multiple_of(u * UW, UW), UW)
            act(pltpu.make_async_copy(dgu_h.at[:, at], RB.at[r], bsem.at[r]))

        @pl.when((u >= 9) & (u < 13))
        def _():
            at = pl.ds(pl.multiple_of((u - 9) * UW, UW), UW)
            act(pltpu.make_async_copy(a_h.at[:, at], RB.at[r], bsem.at[r]))

        @pl.when(u == 13)
        def _():
            act(pltpu.make_async_copy(a_h.at[:, pl.ds(1024, 128)], RB.at[r, :, pl.ds(0, 128)], bsem.at[r]))

    def product(g, left_ref, rhs, w, o0):
        def body(i, _):
            lhs = left_ref[pl.ds(pl.multiple_of(i * 384, 384), 384), :]
            G[g, i, :, :, :, :, o0 : o0 + w] = dot(lhs, rhs).reshape(2, 4, 2, 24, w)
            return 0

        lax.fori_loop(0, 4, body, 0)

    def grads(u):
        g = lax.rem(u, G_SLOTS)

        @pl.when(u >= G_SLOTS)
        def _():
            for n in range(1, 4):
                last_copy(u - G_SLOTS, n).wait_send()

        load(u, lambda copy: copy.wait())

        @pl.when(u < 9)
        def _():
            product(g, n2t, RB[lax.rem(u, 2)], UW, 0)

        @pl.when((u >= 9) & (u < 13))
        def _():
            product(g, dyt, RB[lax.rem(u, 2)], UW, 0)

        @pl.when(u == 13)
        def _():
            product(g, dyt, RB[1, :, 0:128], 128, 0)
            product(g, la, rkv[...], 128, 128)

        @pl.when(u >= 14)
        def _():
            product(g, lb, rq[:, pl.ds(pl.multiple_of((u - 14) * UW, UW), UW)], UW, 0)

        load(u + 2, lambda copy: copy.start())

    def xcopy(i, src, dst, to):
        return remote(src, dst, xss.at[i], xrs.at[i], to)

    def core_copies(base, src):
        return [
            xcopy(base + b, src.at[pl.ds(pl.multiple_of((2 * b + 1 - c) * TOK, TOK), TOK)], C.at[b], core)
            for b in range(2)
        ]

    def local_copies(src):
        return [
            pltpu.make_async_copy(
                src.at[pl.ds(pl.multiple_of((2 * b + c) * TOK, TOK), TOK)], L.at[b], lsem.at[b]
            )
            for b in range(2)
        ]

    def lrow(xx, lo, n):
        return L.at[xx // 2, pl.ds(pl.multiple_of(lax.rem(xx, 2) * HALF + lo, 64), n)]

    x1, x2, x3 = lax.rem(x + 1, 4), lax.rem(x + 2, 4), lax.rem(x + 3, 4)

    def ring1(base):
        return [
            xcopy(base + 2, lrow(x2, 0, 64), S1.at[0], right),
            xcopy(base + 3, lrow(x2, 64, 64), S1.at[1], left),
        ]

    def ring2(base):
        return [
            xcopy(base + 4, lrow(x1, 0, HALF), S2.at[0], right),
            xcopy(base + 5, lrow(x3, 0, HALF), S2.at[1], left),
        ]

    def x_begin(base, src, first):
        if not first:
            pl.semaphore_wait(free.at[0], 1)
        for copy in core_copies(base, src) + local_copies(src):
            copy.start()

    def x_ring1(base, src, first):
        for copy in core_copies(base, src) + local_copies(src):
            copy.wait()

        def add(i, _):
            at = pl.ds(pl.multiple_of(i * 64, 64), 64)
            for b in range(2):
                L[b, at] = L[b, at] + C[b, at]
            return 0

        lax.fori_loop(0, TOK // 64, add, 0)
        if first:
            pl.semaphore_signal(free.at[0], inc=1, device_id=core, device_id_type=MESH)
        else:
            pl.semaphore_wait(free.at[1], 1)
            pl.semaphore_wait(free.at[2], 1)
        for copy in ring1(base):
            copy.start()

    def x_ring2(base):
        for copy in ring1(base):
            copy.wait()
        low, high = lrow(x1, 0, 64), lrow(x3, 64, 64)
        low[...] = low[...] + S1[0]
        high[...] = high[...] + S1[1]
        for copy in ring2(base):
            copy.start()

    def x_end(base, first):
        for copy in ring2(base):
            copy.wait()
        total = lrow(x, 0, HALF)[...] + S2[0] + S2[1]
        if first:
            pl.semaphore_signal(free.at[1], inc=1, device_id=right, device_id_type=MESH)
            pl.semaphore_signal(free.at[2], inc=1, device_id=left, device_id_type=MESH)
        return total

    dh_copy = xcopy(12, dhf.at[mine], dhf.at[mine], mate)
    dh_core = xcopy(13, dhf, dhr, core)
    q_core = xcopy(14, dqf, xqr, core)
    kv_core = xcopy(15, dkvf, xkvr, core)
    dn1_copy = xcopy(16, dn1.at[other], dn1r, mate)
    lo_copy = xcopy(17, lof.at[mine], lof.at[mine], mate)
    di_copy = xcopy(18, dn1.at[mine], dir, mate)

    def second_norm():
        dn2 = x_end(0, True)
        hh = h1[...]
        r2 = lax.rsqrt(mean_last(hh * hh) + EPS)
        normed = hh * r2
        e = dn2 * g2[...]
        grad = cot[mine, :].astype(F32) + r2 * (e - normed * mean_last(e * normed))
        dh[...] = grad
        dhf[mine, :] = grad.astype(BF).astype(F32)
        dh_copy.start()
        small[...] = jnp.zeros_like(small)
        small[0:1, :] = jnp.sum(dn2 * normed, axis=0, keepdims=True)

    def mix_grad():
        dh_copy.wait()
        dh_core.start()
        do[...] = dot_nt(dhf[...].astype(BF), wo[...]).astype(BF)
        dkvf[...] = jnp.zeros_like(dkvf)

    def heads(lo, hi):
        def body(h, _):
            at = pl.ds(pl.multiple_of(h * WIDTH, WIDTH), WIDTH)
            qh, doh = q[:, at], do[:, at]
            s = jnp.where(mask[...] > 0.5, dot_nt(qh, k[...]), NEG_FILL)
            e = jnp.exp(s - jnp.max(s, axis=-1, keepdims=True))
            soft = e / jnp.sum(e, axis=-1, keepdims=True)
            dp = dot_nt(doh, v[...])
            dz = (soft * (dp - jnp.sum(soft * dp, axis=-1, keepdims=True))).astype(BF)
            dq = dot(dz, k[...]) * WIDTH**-0.5
            dqf[:, at] = rope_back(dq, cos[...], sin[...]).astype(BF).astype(F32)
            dkvf[0] = dkvf[0] + dot_tn(dz, qh)
            dkvf[1] = dkvf[1] + dot_tn(soft.astype(BF), doh)
            return 0

        lax.fori_loop(lo, hi, body, 0)

    def head_end():
        dkvf[0] = rope_back(dkvf[0], cos[...], sin[...]).astype(BF).astype(F32)
        dkvf[1] = dkvf[1].astype(BF).astype(F32)
        q_core.start()
        kv_core.start()
        small[2:3, 0:QW] = jnp.sum(dqf[...], axis=0, keepdims=True)
        small[2:3, QW : QW + WIDTH] = jnp.sum(dkvf[0], axis=0, keepdims=True)
        small[2:3, QW + WIDTH : QW + 2 * WIDTH] = jnp.sum(dkvf[1], axis=0, keepdims=True)

    def input_grad():
        dn1[...] = (
            dot_nt(dqf[...].astype(BF), wq[...])
            + dot_nt(dkvf[0].astype(BF), wk[...])
            + dot_nt(dkvf[1].astype(BF), wv[...])
        )
        xf = tokens[...].astype(F32)
        normed = xf * lax.rsqrt(mean_last(xf * xf) + EPS)
        small[1:2, :] = jnp.sum(dn1[...] * normed, axis=0, keepdims=True)
        dn1_copy.start()

    def exchange_end():
        q_core.wait()
        kv_core.wait()
        dh_core.wait()
        rkv[:TOK, :] = dkvf[c].astype(BF)
        rkv[TOK:, :] = xkvr[c].astype(BF)

        @pl.when(c == 0)
        def _():
            rq[:TOK, :] = dqf[...].astype(BF)
            rq[TOK:, :] = xqr[...].astype(BF)
            lb[...] = la[...]

        @pl.when(c == 1)
        def _():
            rq[...] = o2[...]
            lb[:, :TOK] = dhf[...].astype(BF).T
            lb[:, TOK:] = dhr[...].astype(BF).T

    def layer_end():
        lof[mine, :] = (h1[...] + x_end(6, False)).astype(BF).astype(F32)
        lo_copy.start()

    def input_end():
        dn1_copy.wait()
        total = dn1[mine, :] + dn1r[...]
        xf = tokens[mine, :].astype(F32)
        r1 = lax.rsqrt(mean_last(xf * xf) + EPS)
        normed = xf * r1
        e = total * g1[...]
        grad = dh[...] + r1 * (e - normed * mean_last(e * normed))
        dn1[mine, :] = grad.astype(BF).astype(F32)
        di_copy.start()

    def small_copy(i, slot, to):
        return remote(small, sb.at[slot], sss.at[i], srs.at[i], to)

    pair = [small_copy(i, i, to) for i, to in enumerate((mate, core, over))]
    quad_y = [small_copy(3 + i, 3 + y, by_y[i]) for i in range(3)]
    quad_z = [small_copy(6 + i, 7 + z, by_z[i]) for i in range(3)]

    def small_add(i):
        pair[i].wait()
        got = sb[i]
        if i == 0:
            got = jnp.where(lax.broadcasted_iota(jnp.int32, got.shape, 0) < 2, got, 0.0)
        small[...] = small[...] + got

    def small_quad(copies, base, p):
        for copy in copies:
            copy.wait()
        sb[base + p] = small[...]
        small[...] = ((sb[base] + sb[base + 1]) + sb[base + 2]) + sb[base + 3]

    def start(copies):
        for copy in copies:
            copy.start()

    extras = {
        0: [lambda: x_begin(0, dn2_h, True)],
        1: [lambda: x_ring1(0, dn2_h, True)],
        3: [lambda: x_ring2(0)],
        5: [second_norm, lambda: x_begin(6, out_h, False)],
        6: [lambda: x_ring1(6, out_h, False)],
        7: [mix_grad],
        8: [lambda: heads(0, 3)],
        9: [lambda: heads(3, 6), head_end],
        10: [input_grad, lambda: start(pair[:1]), lambda: x_ring2(6)],
        11: [exchange_end, lambda: small_add(0), lambda: start(pair[1:2])],
        12: [layer_end, lambda: small_add(1), lambda: start(pair[2:])],
        13: [input_end, lambda: small_add(2), lambda: start(quad_y)],
        14: [lambda: small_quad(quad_y, 3, y), lambda: start(quad_z)],
        15: [lambda: small_quad(quad_z, 7, z)],
    }

    load(jnp.int32(0), lambda copy: copy.start())
    load(jnp.int32(1), lambda copy: copy.start())
    grads(jnp.int32(0))

    def tick(n, _):
        @pl.when((n >= R_SLOTS) & (n <= NU + 4))
        def _():
            for i in range(4):
                pl.semaphore_wait(credit.at[i], 1)

        @pl.when(n < NU)
        def _():
            for j in range(4):
                step_copy(n, 1, j).start()

        for s in range(1, 7):
            u = n - s
            stage, m = (0, s) if s <= 3 else (1, s - 3)

            @pl.when((u >= 0) & (u < NU))
            def _():
                g, r = lax.rem(u, G_SLOTS), lax.rem(u, R_SLOTS)
                for j in range(4):
                    copy = step_copy(u, s, j)
                    copy.wait_recv()
                    _, p, d = way(j, stage)
                    at = chunk(g, j, stage, lax.rem(p - d * (m + 1) + 8, 4))
                    at[...] = at[...] + (R2 if stage else R1)[r, m - 1, j]
                    if s < 6:
                        step_copy(u, s + 1, j).start()
                    copy.wait_send()
                if s == 6:
                    for i in range(1, 4):
                        last_copy(u, i).start()
                    F[me, u] = G[g, y, xh, z, c]

        @pl.when((n >= 1) & (n <= NU + 5 - R_SLOTS))
        def _():
            for i, to in enumerate((ring["y"][1], ring["y"][0], ring["z"][1], ring["z"][0])):
                pl.semaphore_signal(credit.at[i], inc=1, device_id=to, device_id_type=MESH)

        @pl.when(n + 1 < NU)
        def _():
            grads(n + 1)

        for when, steps in extras.items():

            @pl.when(n == when)
            def _():
                for step in steps:
                    step()

        return 0

    lax.fori_loop(0, N_TICK, tick, 0)

    lo_copy.wait()
    lout_o[...] = lof[...].astype(BF)
    di_copy.wait()
    din_o[mine, :] = dn1[mine, :].astype(BF)
    din_o[other, :] = dir[...].astype(BF)
    small_o[...] = small[...]

    def finish(u, _):
        for n in range(1, 4):
            last_copy(u, n).wait_recv()

            @pl.when(u >= NU - G_SLOTS)
            def _():
                last_copy(u, n).wait_send()

        return 0

    lax.fori_loop(0, NU, finish, 0)

    def tile(i, col):
        return F[i, col // UW, :, col % UW : col % UW + 128]

    for m, out in enumerate((gate_o, up_o, down_o)):
        for i in range(4):
            for n in range(1 if i == 3 else 0, 9):
                out[:, OFFS[i] + 128 * n : OFFS[i] + 128 * (n + 1)] = tile(i, m * FFW + 128 * n)
    base = 3 * FFW
    dk_o[...] = tile(0, base) + tile(2, base)
    dv_o[...] = tile(1, base) + tile(3, base)
    for n in range(HEADS):
        at = slice(128 * n, 128 * (n + 1))
        col = base + 128 * (n + 1)
        dq_o[:, at] = tile(0, col) + tile(2, col)
        dout_o[:, at] = tile(1, col) + tile(3, col)


def back(*args):
    shape = jax.ShapeDtypeStruct
    whole = pl.BlockSpec(memory_space=VM)
    hbm = pl.BlockSpec(memory_space=pl.ANY)
    dma = pltpu.SemaphoreType.DMA
    regular = pltpu.SemaphoreType.REGULAR
    return pl.pallas_call(
        back_kernel,
        name="back",
        out_shape=(
            shape((24, FFL), F32), shape((24, FFL), F32), shape((24, FFL), F32),
            shape((24, QW), F32), shape((24, WIDTH), F32), shape((24, WIDTH), F32), shape((24, QW), F32),
            shape((TOK, D), BF), shape((TOK, D), BF), shape((8, D), F32),
        ),
        in_specs=[whole, whole] + [hbm] * 4 + [whole] * 17,
        out_specs=(whole,) * 10,
        scratch_shapes=[
            VM((4, NU, 24, UW), F32),
            VM((G_SLOTS, 4, 2, 4, 2, 24, UW), F32),
            VM((R_SLOTS, 3, 4, 4, 24, UW), F32),
            VM((R_SLOTS, 3, 4, 24, UW), F32),
            VM((2, 4 * TOK, UW), BF),
            VM((2, TOK, D), F32), VM((2, TOK, D), F32),
            VM((2, HALF // 2, D), F32), VM((2, HALF, D), F32),
            VM((TOK, D), F32), VM((TOK, D), F32), VM((HALF, D), F32), VM((D, 2 * TOK), BF),
            VM((TOK, QW), BF), VM((TOK, QW), F32), VM((TOK, QW), F32), VM((2 * TOK, QW), BF),
            VM((2, TOK, WIDTH), F32), VM((2, TOK, WIDTH), F32), VM((2 * TOK, WIDTH), BF),
            VM((TOK, D), F32), VM((HALF, D), F32), VM((HALF, D), F32), VM((TOK, D), F32),
            VM((8, D), F32), VM((11, 8, D), F32),
            dma((R_SLOTS, 6, 4)), dma((R_SLOTS, 6, 4)), dma((NU, 3)), dma((NU, 3)),
            regular((4,)), dma((19,)), dma((19,)), regular((3,)), dma((2,)), dma((2,)),
            dma((9,)), dma((9,)),
        ],
        compiler_params=pltpu.CompilerParams(
            collective_id=2, has_side_effects=True, vmem_limit_bytes=63 * 2**20
        ),
    )(*args)


def on_device(
    tokens, lengths, keep_mask, norm1_gain, w_query, b_query, w_key, b_key, w_value, b_value,
    w_out, norm2_gain, w_gate, w_up, w_down, cotangent,
):
    inv_freq = ROPE_BASE ** (-jnp.arange(0, WIDTH, 2).astype(F32) / WIDTH)
    inv_freq = jnp.concatenate([inv_freq, inv_freq])[None, :]
    g1 = norm1_gain.astype(F32)[None, :]
    g2 = norm2_gain.astype(F32)[None, :]

    def bias(b):
        return b.astype(F32).reshape(1, -1)

    q, k, v, mask, cos, sin, h1, n2, n2t, dy, dyt, la, o2 = front(
        tokens, cotangent, lengths, keep_mask[None, :], inv_freq, g1, w_query, bias(b_query),
        w_key, bias(b_key), w_value, bias(b_value), w_out, g2,
    )
    dgu, a, dn2_part, out_part = ffn(n2, dy, w_gate, w_up, w_down)
    gate, up, down, dq, dk, dv, dout, layer_out, d_input, small = back(
        n2t, dyt, dgu, a, dn2_part, out_part, la, o2, tokens, cotangent, h1, q, k, v, mask, cos, sin,
        g1, g2, w_query, w_key, w_value, w_out,
    )
    mine = lax.dynamic_slice(small, (0, lax.axis_index("dp") * 24), (8, 24))
    biases = small[2]
    return (
        layer_out,
        d_input,
        mine[1],
        dq,
        biases[:QW].reshape(HEADS, WIDTH),
        dk,
        biases[QW : QW + WIDTH][None, :],
        dv,
        biases[QW + WIDTH : QW + 2 * WIDTH][None, :],
        dout.T,
        mine[0],
        gate,
        up,
        down.T,
    )


def solution(mesh):
    placed = (
        P("dp", None), P("dp", None), P("dp"), P(), P(None, "tensor"), P("tensor", None),
        P(None, "tensor"), P("tensor", None), P(None, "tensor"), P("tensor", None),
        P("tensor", None), P(), P(None, "tensor"), P(None, "tensor"), P("tensor", None), P("dp", None),
    )
    return jax.shard_map(
        on_device,
        mesh=mesh,
        in_specs=placed,
        out_specs=(
            P("dp", None), P("dp", None), P("dp"), P("dp", "tensor"), P("tensor", None),
            P("dp", "tensor"), P("tensor", None), P("dp", "tensor"), P("tensor", None),
            P("tensor", "dp"), P("dp"), P("dp", "tensor"), P("dp", "tensor"), P("tensor", "dp"),
        ),
        check_vma=False,
    )
```

time: 1710 us -> 348 us (0.20)
  waiting for transfers between devices: 1180 us -> 0 us
  Pallas kernels: 0 us -> 327 us
  blocking collectives: 322 us -> 0 us
  matrix products: 133 us -> 0 us
  other arithmetic: 30.7 us -> 3.62 us
    unnamed x15 -> x0, waiting for transfers between devices: 749 us -> none
    pallas_call x0 -> x3, Pallas kernels: none -> 327 us  [the longest x1 205 us: back(): pl.pallas_call(back_kernel, name='back', out_shape=(shape((24, FFL), F32)...]
    unnamed x1 -> x0, blocking collectives: 322 us -> none
    reduce_scatter x2 -> x0, waiting for transfers between devices: 283 us -> none  [the longest x1 160 us: on_device(): lax.psum_scatter(d_query, 'dp', scatter_dimension=0, tiled=True)]
    psum x3 -> x0, waiting for transfers between devices: 149 us -> none  [the longest x1 60.5 us: on_device(): lax.psum(jnp.dot(attn_mix, w_out, preferred_element_type=jnp.float32), 't...]
    dot_general x27 -> x0, matrix products: 133 us -> none  [the longest x7 47 us: weight_grad(): jnp.einsum('tc,ti->ci', left, right, preferred_element_type=jnp.float32)]
  transfers between devices with their start and end apart: 10 -> 0, of which waited for: 8 -> 0; matrix products, arithmetic and copies ran while one was open for 4% -> 0% of each run, Pallas kernels for 0% -> 0%
where the time goes in v1:
time: 348 us
  Pallas kernels  327 us (94%)
  local copies, waits for them, and re-layouts  16 us (5%)
  other arithmetic  3.62 us (1%)
    pallas_call x1, Pallas kernels, back(): pl.pallas_call(back_kernel, name='back', out_shape=(shape((24, FFL), F32)...  205 us
    pallas_call x1, Pallas kernels, front(): pl.pallas_call(front_kernel, name='front', out_shape=(shape((TOK, QW), BF...  84 us
    pallas_call x1, Pallas kernels, ffn(): pl.pallas_call(ffn_kernel, name='ffn', out_shape=(shape((4 * TOK, 2 * FFW...  38 us
    unnamed x24, local copies, waits for them, and re-layouts  9.48 us

profile of v1, /device:TPU:1, one launch (start us, length us, event | category | flops | bytes accessed | tf_op | source)
XLA Modules:
  0.0 347.5 jit_solution(6306742864248902744)
XLA Ops:
  0.6 1.3 reshape.45.g1
  1.9 1.3 reshape.48.g2
  3.2 0.7 convert_bitcast_fusion
  3.9 0.6 copy.32
  4.5 0.6 maximum_bitcast_fusion.inv_freq
  5.1 1.2 convert_element_type.15.bk
  6.2 1.2 convert_element_type.16.bv
  7.4 84.0 %front.1 = (bf16[256,768]{1,0:T(8,128)(2,1)}, bf16[256,128]{1,0:T(8,128)(2,1)}, bf16[256,128]{1,0:T(8,128)(2,1)}, f32[256,256]{1,0:T(8,128)}, f32[256,128]{1,0:T...) custom-call(bf16[256,1536]{1,0:T(8,128)(2,1)} %tokens.3, ...), custom_call_target="tpu_custom_call" | custom-call | tf_op jit(solution)/shard_map/front/pallas_call | solution.py:249
  91.4 38.0 %ffn.1 = (bf16[1024,2304]{1,0:T(8,128)(2,1)}, bf16[1024,1152]{1,0:T(8,128)(2,1)}, f32[1024,1536]{1,0:T(8,128)}, f32[1024,1536]{1,0:T(8,128)}) custom-call(bf16[1024,1536]{1,0:T(8,128)(2,1)} %get-tuple-element.43.n2, bf16[1024,1536]{1,0:T(8,128)(2,1)} %get-tuple-element.44.dy, bf16[1536,4480]{1,0:T(8,128)(2,1)} %wg_hbm.1, bf16[1536,4480]{1,0:T(8,128)(2,1)} %wu_hbm.1, ...), custom_call_target="tpu_custom_call" | custom-call | tf_op jit(solution)/shard_map/ffn/pallas_call | solution.py:316
  129.5 205.1 %back.1 = (f32[24,4480]{1,0:T(8,128)}, f32[24,4480]{1,0:T(8,128)}, f32[24,4480]{1,0:T(8,128)}, f32[24,768]{1,0:T(8,128)}, f32[24,128]{1,0:T(8,128)}, /*index=5*/...) custom-call(bf16[1536,1024]{1,0:T(8,128)(2,1)} %get-tuple-element.41, ...), custom_call_target="tpu_custom_call" | custom-call | tf_op jit(solution)/shard_map/back/pallas_call | solution.py:758
  334.6 0.0 copy-start.4
  334.6 0.0 copy-start.6
  334.6 0.0 copy-start.5
  334.6 0.0 copy-start.3
  334.6 0.0 copy-start.2
  334.7 0.0 copy-start.1
  334.7 0.0 copy-start
  334.7 0.9 constant_dynamic-slice_fusion
  335.6 0.5 slice_bitcast_fusion
  336.1 1.3 slice_reduce_fusion
  337.4 1.2 fusion
  338.6 2.1 copy.42
  340.7 2.1 copy.43
  342.7 0.0 copy-done.4
  342.8 0.6 copy.44
  343.4 0.0 copy-done.6
  343.4 0.6 copy.45
  344.0 0.0 copy-done.5
  344.0 0.6 copy.46
  344.6 0.0 copy-done.3
  344.6 0.6 copy.47
  345.2 0.0 copy-done.2
  345.2 0.8 copy.48
  346.0 0.0 copy-done.1
  346.0 0.8 copy.49
  346.7 0.0 copy-done
  346.7 0.8 copy.50
  (1 shorter events, 0.0 us)
Async XLA Ops:
  334.6 8.1 %copy-start.4 = (f32[24,768]{1,0:T(8,128)S(1)}, f32[24,768]{1,0:T(8,128)}, u32[]{:S(2)}) copy-start(f32[24,768]{1,0:T(8,128)} %get-tuple-element.89) | copy-start | bytes 221188
  334.6 8.8 %copy-start.6 = (f32[24,128]{1,0:T(8,128)S(1)}, f32[24,128]{1,0:T(8,128)}, u32[]{:S(2)}) copy-start(f32[24,128]{1,0:T(8,128)} %get-tuple-element.91) | copy-start | bytes 36868
  334.6 9.4 %copy-start.5 = (f32[24,128]{1,0:T(8,128)S(1)}, f32[24,128]{1,0:T(8,128)}, u32[]{:S(2)}) copy-start(f32[24,128]{1,0:T(8,128)} %get-tuple-element.93) | copy-start | bytes 36868
  334.6 10.0 %copy-start.3 = (f32[24,768]{1,0:T(8,128)S(1)}, f32[24,768]{1,0:T(8,128)}, u32[]{:S(2)}) copy-start(f32[24,768]{1,0:T(8,128)} %get-tuple-element.64) | copy-start | bytes 221188
  334.6 10.6 %copy-start.2 = (f32[24,4480]{1,0:T(8,128)S(1)}, f32[24,4480]{1,0:T(8,128)}, u32[]{:S(2)}) copy-start(f32[24,4480]{1,0:T(8,128)} %get-tuple-element.97) | copy-start | bytes 1290244
  334.7 11.3 %copy-start.1 = (f32[24,4480]{1,0:T(8,128)S(1)}, f32[24,4480]{1,0:T(8,128)}, u32[]{:S(2)}) copy-start(f32[24,4480]{1,0:T(8,128)} %get-tuple-element.98) | copy-start | bytes 1290244
  334.7 12.1 %copy-start = (f32[24,4480]{1,0:T(8,128)S(1)}, f32[24,4480]{1,0:T(8,128)}, u32[]{:S(2)}) copy-start(f32[24,4480]{1,0:T(8,128)} %get-tuple-element.67) | copy-start | bytes 1290244

commit v2 on v1

--- a/solution.py
+++ b/solution.py
@@ -1,4 +1,4 @@
-import functools
+import math
 
 import jax
 import jax.numpy as jnp
@@ -28,9 +28,9 @@
 UW = 256
 NU = 17
 GATE_UNITS = 9
-G_SLOTS = 8
+G_SLOTS = 7
 R_SLOTS = 3
-N_TICK = NU + 6
+N_TICK = NU + 4
 
 
 def coords():
@@ -85,19 +85,21 @@
 
 
 def front_kernel(
-    tokens, cot, lengths, keep, inv_freq, g1, wq, bq, wk, bk, wv, bv, wo, g2,
-    q_o, k_o, v_o, mask_o, cos_o, sin_o, h1_o, n2_o, n2t_o, dy_o, dyt_o, la_o, o2_o,
-    n2f, dyf, n1f, n1r, of, orr, part, prec, ss, rs,
+    tokens, cot, lengths, keep, g1, wq, bq, wk, bk, wv, bv, wo, g2, wg_h, wu_h, wd_h,
+    q_o, k_o, v_o, mask_o, cos_o, sin_o, h1_o, la_o, o2_o,
+    n2t_h, dyt_h, dgu_h, a_h, dn2_h, out_h,
+    n2f, dyf, n1f, n1r, of, orr, part, prec, wg, wu, wd, n2t_s, dyt_s, dgu_s, a_s, dn2_s, out_s,
+    ss, rs, wsem, osem, tsem,
 ):
     y, xh, z, c, t = coords()
     x = 2 * xh + t
-    right = device_x(y, lax.rem(x + 1, 4), z, c)
-    left = device_x(y, lax.rem(x + 3, 4), z, c)
+    x1, x2, x3 = lax.rem(x + 1, 4), lax.rem(x + 2, 4), lax.rem(x + 3, 4)
+    right = device_x(y, x1, z, c)
+    left = device_x(y, x3, z, c)
     core = device(y, xh, z, 1 - c, t)
     mate = device(y, xh, z, c, 1 - t)
     cross = device_x(y, 3 - x, z, c)
     greet((right, left, core))
-    me = 2 * xh + c
     mine = pl.ds(pl.multiple_of(t * HALF, HALF), HALF)
     other = pl.ds(pl.multiple_of((1 - t) * HALF, HALF), HALF)
 
@@ -106,14 +108,26 @@
         copy.start()
         return copy
 
-    dyf[me] = cot[...].astype(F32)
-    dy_cross = send(0, dyf.at[me, mine], dyf.at[me, mine], cross)
-    dy_core = send(1, dyf.at[me], dyf.at[me], core)
+    near = pl.ds(2 * xh, 2)
+    far = pl.ds(2 * (1 - xh), 2)
+    dyf[near, c] = cot[...].astype(F32).reshape(2, HALF, D)
+    dy_cross = send(0, dyf.at[near, c], dyf.at[near, c], cross)
+    dy_core = send(1, dyf.at[near, c], dyf.at[near, c], core)
+
+    me = 2 * xh + c
+    hidden = pl.ds(pl.multiple_of((me * 9 - me // 3) * 128, 128), FFW)
+    loads = [
+        pltpu.make_async_copy(wg_h.at[:, hidden], wg, wsem.at[0]),
+        pltpu.make_async_copy(wu_h.at[:, hidden], wu, wsem.at[1]),
+        pltpu.make_async_copy(wd_h.at[hidden, :], wd, wsem.at[2]),
+    ]
+    for copy in loads:
+        copy.start()
 
     rows = lax.broadcasted_iota(jnp.int32, (TOK, TOK), 0)
     cols = lax.broadcasted_iota(jnp.int32, (TOK, TOK), 1)
-    place = lax.broadcasted_iota(jnp.int32, (TOK, WIDTH), 0)
-    row_id = place
+    row_id = lax.broadcasted_iota(jnp.int32, (TOK, WIDTH), 0)
+    place = row_id
     seg_r = jnp.zeros((TOK, TOK), jnp.int32)
     seg_c = jnp.zeros((TOK, TOK), jnp.int32)
     end = jnp.int32(0)
@@ -125,24 +139,27 @@
         place = place - jnp.where(row_id >= end, span, 0)
     allowed = (seg_r == seg_c) & (cols <= rows) & ((keep[...] == 1) | (cols == rows))
     mask_o[...] = allowed.astype(F32)
-    angle = place.astype(F32) * inv_freq[...]
     lane = lax.broadcasted_iota(jnp.int32, (TOK, WIDTH), 1)
+    first = lane < WIDTH // 2
+    step = jnp.where(first, lane, lane - WIDTH // 2).astype(F32)
+    angle = place.astype(F32) * jnp.exp(step * (-2.0 * math.log(ROPE_BASE) / WIDTH))
     cosine = jnp.cos(angle)
-    sine = jnp.sin(angle) * jnp.where(lane < WIDTH // 2, -1.0, 1.0)
+    sine = jnp.sin(angle) * jnp.where(first, -1.0, 1.0)
     cos_o[...] = cosine
     sin_o[...] = sine
 
     xf = tokens[...].astype(F32)
     r1 = lax.rsqrt(mean_last(xf * xf) + EPS)
-    n1 = (xf * r1 * g1[...]).astype(BF)
+    n1 = (xf * r1 * g1[...].astype(F32)).astype(BF)
     n1f[...] = n1.astype(F32)
     n1_core = send(2, n1f, n1r, core)
-    kp = dot(n1, wk[...]) + bk[...]
+    kp = dot(n1, wk[...]) + bk[...].astype(F32)
     k_o[...] = rope(kp, cosine, sine).astype(BF)
-    v_o[...] = (dot(n1, wv[...]) + bv[...]).astype(BF)
+    v_o[...] = (dot(n1, wv[...]) + bv[...].astype(F32)).astype(BF)
+    bias = bq[...].astype(F32)
     for h in range(HEADS):
         at = slice(h * WIDTH, (h + 1) * WIDTH)
-        qp = dot(n1, wq[:, at]) + bq[:, at]
+        qp = dot(n1, wq[:, at]) + bias[h : h + 1]
         q_o[:, at] = (rope(qp, cosine, sine) * WIDTH**-0.5).astype(BF)
 
     def head(h, _):
@@ -160,84 +177,117 @@
     half = send(3, part.at[0], prec, mate)
     o_core = send(4, of, orr, core)
     part[1] = dot(o2_o[mine, :], wo[...])
-
-    dy_cross.wait_recv()
-    far = 2 * (1 - xh) + c
-    dy_pass = send(5, dyf.at[far, other], dyf.at[far, other], mate)
-
-    half.wait_recv()
-    h1 = tokens[mine, :].astype(F32) + part[1] + prec[...]
-    h1_o[...] = h1
-    r2 = lax.rsqrt(mean_last(h1 * h1) + EPS)
-    n2f[me, mine] = (h1 * r2 * g2[...]).astype(BF).astype(F32)
-
-    own = n2f.at[me, mine]
-    to_right = send(6, own, own, right)
-    to_left = send(7, own, own, left)
-    to_core = send(8, own, own, core)
-
     la_o[:, :TOK] = n1.T
     n1_core.wait_recv()
     la_o[:, TOK:] = n1r[...].astype(BF).T
     o_core.wait_recv()
     o2_o[TOK:, :] = orr[...].astype(BF)
 
-    def dy_block(b):
-        low = dyf[b].astype(BF)
-        at = pl.ds(pl.multiple_of(b * TOK, TOK), TOK)
-        dy_o[at, :] = low
-        dyt_o[:, at] = low.T
-
-    dy_block(me)
+    half.wait_recv()
+    h1 = tokens[mine, :].astype(F32) + part[1] + prec[...]
+    h1_o[...] = h1
+    r2 = lax.rsqrt(mean_last(h1 * h1) + EPS)
+    n2f[x, c] = (h1 * r2 * g2[...].astype(F32)).astype(BF).astype(F32)
+
+    def pass_on(i, xx, to, lo=0, n=HALF):
+        at = n2f.at[xx, c, pl.ds(lo, n)]
+        return send(i, at, at, to)
+
+    to_right = pass_on(5, x, right)
+    to_left = pass_on(6, x, left)
+    to_core = pass_on(7, x, core)
+
+    unit = lax.broadcasted_iota(jnp.int32, (1, FFW), 1)
+    live = jnp.where((unit < 128) & (me == 3), 0.0, 1.0)
+
+    def tokens_of(xx):
+        return pl.ds(pl.multiple_of(xx * TOK, TOK), TOK)
+
+    def results(n, xx):
+        slot, at = n % 2, tokens_of(xx)
+        return [
+            pltpu.make_async_copy(src, dst, osem.at[slot, i])
+            for i, (src, dst) in enumerate((
+                (n2t_s.at[slot], n2t_h.at[:, at]),
+                (dgu_s.at[slot], dgu_h.at[at]),
+                (a_s.at[slot], a_h.at[at]),
+                (dn2_s.at[slot], dn2_h.at[xx]),
+                (out_s.at[slot], out_h.at[xx]),
+            ))
+        ]
+
+    order = (x, x3, x1, x2)
+
+    def feed(n):
+        xx, slot = order[n], n % 2
+        if n >= 2:
+            for copy in results(n - 2, order[n - 2]):
+                copy.wait()
+        here = n2f[xx].reshape(TOK, D).astype(BF)
+        g = dot(here, wg[...])
+        u = dot(here, wu[...])
+        n2t_s[slot] = here.T
+        sg = live / (1.0 + jnp.exp(-g))
+        silu = g * sg
+        a = (silu * u).astype(BF)
+        a_s[slot] = a
+        out_s[slot] = dot(a, wd[...]).reshape(2, HALF, D)
+        da = dot_nt(dyf[xx].reshape(TOK, D).astype(BF), wd[...])
+        dg = (da * u * sg * (1.0 + g * (1.0 - sg))).astype(BF)
+        du = (da * silu).astype(BF)
+        dgu_s[slot, :, :FFW] = dg
+        dgu_s[slot, :, FFW:] = du
+        dn2_s[slot] = (dot_nt(dg, wg[...]) + dot_nt(du, wu[...])).reshape(2, HALF, D)
+        for copy in results(n, xx):
+            copy.start()
+
+    def turned(n, xx):
+        return pltpu.make_async_copy(dyt_s.at[n % 2], dyt_h.at[:, tokens_of(xx)], tsem.at[n % 2])
+
+    around = (x, 2 * xh + 1 - t, x2, 3 - x)
+
+    def turn(n):
+        xx = around[n]
+        if n >= 2:
+            turned(n - 2, around[n - 2]).wait()
+        dyt_s[n % 2] = dyf[xx].reshape(TOK, D).astype(BF).T
+        turned(n, xx).start()
+
     dy_core.wait_recv()
-    dy_block(2 * xh + 1 - c)
-
-    def slot(xx):
-        return n2f.at[2 * (xx // 2) + c, pl.ds(pl.multiple_of(lax.rem(xx, 2) * HALF, HALF), HALF)]
-
-    def lower(ref):
-        return ref.at[pl.ds(0, HALF // 2)]
-
-    def upper(ref):
-        return ref.at[pl.ds(HALF // 2, HALF // 2)]
-
-    from_left = slot(lax.rem(x + 3, 4))
-    from_right = slot(lax.rem(x + 1, 4))
+    to_core.wait_recv()
+    for copy in loads:
+        copy.wait()
+    feed(0)
+    turn(0)
+    turn(1)
+    dy_cross.wait_recv()
+    dy_far = send(8, dyf.at[far, c], dyf.at[far, c], core)
+
     to_right.wait_recv()
-    pass_right = send(9, lower(from_left), lower(from_left), right)
-    core_left = send(10, from_left, from_left, core)
+    pass_right = pass_on(9, x3, right, 0, HALF // 2)
+    core_left = pass_on(10, x3, core)
     to_left.wait_recv()
-    pass_left = send(11, upper(from_right), upper(from_right), left)
-    core_right = send(12, from_right, from_right, core)
-
-    dy_pass.wait_recv()
-    dy_far = send(13, dyf.at[far], dyf.at[far], core)
-    dy_block(far)
-
+    pass_left = pass_on(11, x1, left, HALF // 2, HALF // 2)
+    core_right = pass_on(12, x1, core)
+    dy_far.wait_recv()
+    core_left.wait_recv()
+    feed(1)
     pass_right.wait_recv()
     pass_left.wait_recv()
-    across = slot(lax.rem(x + 2, 4))
-    core_across = send(14, across, across, core)
-    dy_far.wait_recv()
-    dy_block(2 * (1 - xh) + 1 - c)
-
-    def n2_block(b):
-        low = n2f[b].astype(BF)
-        at = pl.ds(pl.multiple_of(b * TOK, TOK), TOK)
-        n2_o[at, :] = low
-        n2t_o[:, at] = low.T
-
-    n2_block(me)
-    n2_block(far)
-    to_core.wait_recv()
-    core_left.wait_recv()
+    core_across = pass_on(13, x2, core)
     core_right.wait_recv()
+    feed(2)
+    turn(2)
+    turn(3)
     core_across.wait_recv()
-    n2_block(2 * xh + 1 - c)
-    n2_block(2 * (1 - xh) + 1 - c)
+    feed(3)
+    for n in (2, 3):
+        turned(n, around[n]).wait()
+        for copy in results(n, order[n]):
+            copy.wait()
     for copy in (
-        dy_cross, dy_core, n1_core, half, o_core, dy_pass, to_right, to_left, to_core,
-        pass_right, core_left, pass_left, core_right, dy_far, core_across,
+        dy_cross, dy_core, n1_core, half, o_core, to_right, to_left, to_core,
+        dy_far, pass_right, core_left, pass_left, core_right, core_across,
     ):
         copy.wait_send()
 
@@ -246,86 +296,35 @@
     shape = jax.ShapeDtypeStruct
     whole = pl.BlockSpec(memory_space=VM)
     scalars = pl.BlockSpec(memory_space=pltpu.SMEM)
+    hbm = pl.BlockSpec(memory_space=pl.ANY)
+    dma = pltpu.SemaphoreType.DMA
     return pl.pallas_call(
         front_kernel,
         name="front",
         out_shape=(
             shape((TOK, QW), BF), shape((TOK, WIDTH), BF), shape((TOK, WIDTH), BF),
             shape((TOK, TOK), F32), shape((TOK, WIDTH), F32), shape((TOK, WIDTH), F32),
-            shape((HALF, D), F32),
-            shape((4 * TOK, D), BF), shape((D, 4 * TOK), BF),
-            shape((4 * TOK, D), BF), shape((D, 4 * TOK), BF),
-            shape((D, 2 * TOK), BF), shape((2 * TOK, QW), BF),
+            shape((HALF, D), F32), shape((D, 2 * TOK), BF), shape((2 * TOK, QW), BF),
+            shape((D, 4 * TOK), BF), shape((D, 4 * TOK), BF),
+            shape((4 * TOK, 2 * FFW), BF), shape((4 * TOK, FFW), BF),
+            shape((4, 2, HALF, D), F32), shape((4, 2, HALF, D), F32),
         ),
-        in_specs=[whole, whole, scalars] + [whole] * 11,
-        out_specs=(whole,) * 13,
+        in_specs=[whole, whole, scalars] + [whole] * 10 + [hbm] * 3,
+        out_specs=(whole,) * 9 + (hbm,) * 6,
         scratch_shapes=[
-            VM((4, TOK, D), F32), VM((4, TOK, D), F32),
+            VM((4, 2, HALF, D), F32), VM((4, 2, HALF, D), F32),
             VM((TOK, D), F32), VM((TOK, D), F32),
             VM((TOK, QW), F32), VM((TOK, QW), F32),
             VM((2, HALF, D), F32), VM((HALF, D), F32),
-            pltpu.SemaphoreType.DMA((15,)), pltpu.SemaphoreType.DMA((15,)),
+            VM((D, FFW), BF), VM((D, FFW), BF), VM((FFW, D), BF),
+            VM((2, D, TOK), BF), VM((2, D, TOK), BF),
+            VM((2, TOK, 2 * FFW), BF), VM((2, TOK, FFW), BF),
+            VM((2, 2, HALF, D), F32), VM((2, 2, HALF, D), F32),
+            dma((14,)), dma((14,)), dma((3,)), dma((2, 5)), dma((2,)),
         ],
         compiler_params=pltpu.CompilerParams(
-            collective_id=1, has_side_effects=True, vmem_limit_bytes=60 * 2**20
+            collective_id=1, has_side_effects=True, vmem_limit_bytes=63 * 2**20
         ),
-    )(*args)
-
-
-def ffn_kernel(n2, dy, wg_hbm, wu_hbm, wd_hbm, dgu_o, a_o, dn2_o, out_o, wg, wu, wd, sem):
-    _, xh, _, c, _ = coords()
-    me = 2 * xh + c
-    start = pl.multiple_of((me * 9 - me // 3) * 128, 128)
-    at = pl.ds(start, FFW)
-    copies = [
-        pltpu.make_async_copy(wg_hbm.at[:, at], wg, sem.at[0]),
-        pltpu.make_async_copy(wu_hbm.at[:, at], wu, sem.at[1]),
-        pltpu.make_async_copy(wd_hbm.at[at, :], wd, sem.at[2]),
-    ]
-    for copy in copies:
-        copy.start()
-    lane = lax.broadcasted_iota(jnp.int32, (1, FFW), 1)
-    live = jnp.where((lane < 128) & (me == 3), 0.0, 1.0)
-    for copy in copies:
-        copy.wait()
-
-    def block(i, _):
-        rows = pl.ds(pl.multiple_of(i * TOK, TOK), TOK)
-        g = dot(n2[rows, :], wg[...])
-        u = dot(n2[rows, :], wu[...])
-        sg = live / (1.0 + jnp.exp(-g))
-        silu = g * sg
-        a = (silu * u).astype(BF)
-        a_o[rows, :] = a
-        da = dot_nt(dy[rows, :], wd[...])
-        dg = (da * u * sg * (1.0 + g * (1.0 - sg))).astype(BF)
-        du = (da * silu).astype(BF)
-        dgu_o[rows, :FFW] = dg
-        dgu_o[rows, FFW:] = du
-        dn2_o[rows, :] = dot_nt(dg, wg[...]) + dot_nt(du, wu[...])
-        out_o[rows, :] = dot(a, wd[...])
-        return 0
-
-    lax.fori_loop(0, 4, block, 0)
-
-
-def ffn(*args):
-    shape = jax.ShapeDtypeStruct
-    whole = pl.BlockSpec(memory_space=VM)
-    hbm = pl.BlockSpec(memory_space=pl.ANY)
-    return pl.pallas_call(
-        ffn_kernel,
-        name="ffn",
-        out_shape=(
-            shape((4 * TOK, 2 * FFW), BF), shape((4 * TOK, FFW), BF),
-            shape((4 * TOK, D), F32), shape((4 * TOK, D), F32),
-        ),
-        in_specs=[whole, whole, hbm, hbm, hbm],
-        out_specs=(whole,) * 4,
-        scratch_shapes=[
-            VM((D, FFW), BF), VM((D, FFW), BF), VM((FFW, D), BF), pltpu.SemaphoreType.DMA((3,)),
-        ],
-        compiler_params=pltpu.CompilerParams(vmem_limit_bytes=60 * 2**20),
     )(*args)
 
 
@@ -333,7 +332,7 @@
     n2t, dyt, dgu_h, a_h, dn2_h, out_h, la, o2, tokens, cot, h1, q, k, v, mask, cos, sin,
     g1, g2, wq, wk, wv, wo,
     gate_o, up_o, down_o, dq_o, dk_o, dv_o, dout_o, lout_o, din_o, small_o,
-    F, G, R1, R2, RB, C, L, S1, S2, dhf, dhr, dh, lb, do, dqf, xqr, rq, dkvf, xkvr, rkv,
+    F, G, R1, R2, R3, R4, RB, C, L, S1, S2, dhf, dhr, dh, lb, do, dqf, xqr, rq, dkvf, xkvr, rkv,
     dn1, dn1r, dir, lof, small, sb,
     ss, rs, fss, frs, credit, xss, xrs, free, lsem, bsem, sss, srs,
 ):
@@ -354,38 +353,61 @@
     mine = pl.ds(pl.multiple_of(t * HALF, HALF), HALF)
     other = pl.ds(pl.multiple_of((1 - t) * HALF, HALF), HALF)
 
-    def way(j, stage):
-        axis = "y" if (j // 2 == 0) == (stage == 0) else "z"
-        return axis, (y if axis == "y" else z), (1 if j % 2 == 0 else -1)
-
-    def chunk(g, j, stage, i):
-        jx, jc = j // 2, j % 2
-        if stage == 0:
-            return G.at[g, i, 0, :, jc] if jx == 0 else G.at[g, :, 1, i, jc]
-        return G.at[g, y, 0, i, jc] if jx == 0 else G.at[g, i, 1, z, jc]
-
-    def step_copy(u, s, j):
-        stage, n = (0, s) if s <= 3 else (1, s - 3)
-        axis, p, d = way(j, stage)
+    R = (R1, R2, R3, R4)
+
+    def axis(j, s):
+        return ("y", y) if (j == 0) == (s <= 2) else ("z", z)
+
+    def part(g, j, s, i, way):
+        own = z if j else y
+        if s == 1:
+            return G.at[g, j, i, way]
+        if s == 2:
+            return G.at[g, j, i]
+        return G.at[g, j, own, way, i] if s == 3 else G.at[g, j, own, :, i]
+
+    def step_copy(u, s, j, way):
+        name, p = axis(j, s)
         g, r = lax.rem(u, G_SLOTS), lax.rem(u, R_SLOTS)
+        to = lax.rem(p + (2 if s % 2 else (3 if way else 1)), 4)
         return remote(
-            chunk(g, j, stage, lax.rem(p - d * n + 8, 4)),
-            (R2 if stage else R1).at[r, n - 1, j],
-            ss.at[r, s - 1, j],
-            rs.at[r, s - 1, j],
-            ring[axis][0 if d == 1 else 1],
+            part(g, j, s, to, way),
+            R[s - 1].at[r, j, way],
+            ss.at[r, s - 1, j, way],
+            rs.at[r, s - 1, j, way],
+            ring[name][way],
         )
+
+    def total(u, px, pc):
+        return G.at[lax.rem(u, G_SLOTS), px, jnp.where(px == 0, y, z), pc, jnp.where(px == 0, z, y)]
 
     def last_copy(u, n):
         px = 1 - xh if n & 2 else xh
         pc = 1 - c if n & 1 else c
-        return remote(
-            G.at[lax.rem(u, G_SLOTS), y, px, z, pc],
-            F.at[me, u],
-            fss.at[u, n - 1],
-            frs.at[u, n - 1],
-            peers[n],
-        )
+        return remote(total(u, px, pc), F.at[me, u], fss.at[u, n - 1], frs.at[u, n - 1], peers[n])
+
+    def advance(u, s):
+        g, r = lax.rem(u, G_SLOTS), lax.rem(u, R_SLOTS)
+        for j in range(2):
+            _, p = axis(j, s)
+            for way in range(2):
+                step_copy(u, s, j, way).wait_recv()
+                if s % 2:
+                    at = part(g, j, s, lax.rem(p + (3 if way else 1), 4), way)
+                    at[...] = at[...] + R[s - 1][r, j, way]
+                    step_copy(u, s + 1, j, way).start()
+            if s % 2 == 0:
+                at = part(g, j, s, p, 0)
+                at[...] = at[...] + R[s - 1][r, j, 0] + R[s - 1][r, j, 1]
+                if s == 2:
+                    for way in range(2):
+                        step_copy(u, 3, j, way).start()
+            for way in range(2):
+                step_copy(u, s, j, way).wait_send()
+        if s == 4:
+            for n in range(1, 4):
+                last_copy(u, n).start()
+            F[me, u] = total(u, xh, c)[...]
 
     def load(u, act):
         r = lax.rem(u, 2)
@@ -407,7 +429,11 @@
     def product(g, left_ref, rhs, w, o0):
         def body(i, _):
             lhs = left_ref[pl.ds(pl.multiple_of(i * 384, 384), 384), :]
-            G[g, i, :, :, :, :, o0 : o0 + w] = dot(lhs, rhs).reshape(2, 4, 2, 24, w)
+            res = dot(lhs, rhs).reshape(2, 4, 2, 24, w)
+            for zz in range(4):
+                for cc in range(2):
+                    G[g, 0, i, cc, zz, :, o0 : o0 + w] = res[0, zz, cc]
+                    G[g, 1, zz, cc, i, :, o0 : o0 + w] = res[1, zz, cc]
             return 0
 
         lax.fori_loop(0, 4, body, 0)
@@ -444,22 +470,14 @@
     def xcopy(i, src, dst, to):
         return remote(src, dst, xss.at[i], xrs.at[i], to)
 
-    def core_copies(base, src):
-        return [
-            xcopy(base + b, src.at[pl.ds(pl.multiple_of((2 * b + 1 - c) * TOK, TOK), TOK)], C.at[b], core)
-            for b in range(2)
-        ]
-
-    def local_copies(src):
-        return [
-            pltpu.make_async_copy(
-                src.at[pl.ds(pl.multiple_of((2 * b + c) * TOK, TOK), TOK)], L.at[b], lsem.at[b]
-            )
-            for b in range(2)
-        ]
+    def core_copy(base, src):
+        return xcopy(base, src.at[:, 1 - c], C, core)
+
+    def local_copy(src):
+        return pltpu.make_async_copy(src.at[:, c], L, lsem.at[0])
 
     def lrow(xx, lo, n):
-        return L.at[xx // 2, pl.ds(pl.multiple_of(lax.rem(xx, 2) * HALF + lo, 64), n)]
+        return L.at[xx, pl.ds(lo, n)]
 
     x1, x2, x3 = lax.rem(x + 1, 4), lax.rem(x + 2, 4), lax.rem(x + 3, 4)
 
@@ -478,20 +496,18 @@
     def x_begin(base, src, first):
         if not first:
             pl.semaphore_wait(free.at[0], 1)
-        for copy in core_copies(base, src) + local_copies(src):
-            copy.start()
+        core_copy(base, src).start()
+        local_copy(src).start()
 
     def x_ring1(base, src, first):
-        for copy in core_copies(base, src) + local_copies(src):
-            copy.wait()
+        core_copy(base, src).wait()
+        local_copy(src).wait()
 
         def add(i, _):
-            at = pl.ds(pl.multiple_of(i * 64, 64), 64)
-            for b in range(2):
-                L[b, at] = L[b, at] + C[b, at]
+            L[i] = L[i] + C[i]
             return 0
 
-        lax.fori_loop(0, TOK // 64, add, 0)
+        lax.fori_loop(0, 4, add, 0)
         if first:
             pl.semaphore_signal(free.at[0], inc=1, device_id=core, device_id_type=MESH)
         else:
@@ -531,7 +547,7 @@
         hh = h1[...]
         r2 = lax.rsqrt(mean_last(hh * hh) + EPS)
         normed = hh * r2
-        e = dn2 * g2[...]
+        e = dn2 * g2[...].astype(F32)
         grad = cot[mine, :].astype(F32) + r2 * (e - normed * mean_last(e * normed))
         dh[...] = grad
         dhf[mine, :] = grad.astype(BF).astype(F32)
@@ -580,6 +596,7 @@
         xf = tokens[...].astype(F32)
         normed = xf * lax.rsqrt(mean_last(xf * xf) + EPS)
         small[1:2, :] = jnp.sum(dn1[...] * normed, axis=0, keepdims=True)
+        small_mate.start()
         dn1_copy.start()
 
     def exchange_end():
@@ -611,7 +628,7 @@
         xf = tokens[mine, :].astype(F32)
         r1 = lax.rsqrt(mean_last(xf * xf) + EPS)
         normed = xf * r1
-        e = total * g1[...]
+        e = total * g1[...].astype(F32)
         grad = dh[...] + r1 * (e - normed * mean_last(e * normed))
         dn1[mine, :] = grad.astype(BF).astype(F32)
         di_copy.start()
@@ -619,16 +636,15 @@
     def small_copy(i, slot, to):
         return remote(small, sb.at[slot], sss.at[i], srs.at[i], to)
 
-    pair = [small_copy(i, i, to) for i, to in enumerate((mate, core, over))]
-    quad_y = [small_copy(3 + i, 3 + y, by_y[i]) for i in range(3)]
-    quad_z = [small_copy(6 + i, 7 + z, by_z[i]) for i in range(3)]
-
-    def small_add(i):
-        pair[i].wait()
-        got = sb[i]
-        if i == 0:
-            got = jnp.where(lax.broadcasted_iota(jnp.int32, got.shape, 0) < 2, got, 0.0)
-        small[...] = small[...] + got
+    small_mate = small_copy(0, 0, mate)
+    quad_y = [small_copy(1 + i, 1 + y, by_y[i]) for i in range(3)]
+    quad_z = [small_copy(4 + i, 5 + z, by_z[i]) for i in range(3)]
+    quad_x = [small_copy(6 + i, 9 + me, peers[i]) for i in range(1, 4)]
+
+    def small_add():
+        small_mate.wait()
+        gains = lax.broadcasted_iota(jnp.int32, small.shape, 0) < 2
+        small[...] = small[...] + jnp.where(gains, sb[0], 0.0)
 
     def small_quad(copies, base, p):
         for copy in copies:
@@ -645,16 +661,15 @@
         1: [lambda: x_ring1(0, dn2_h, True)],
         3: [lambda: x_ring2(0)],
         5: [second_norm, lambda: x_begin(6, out_h, False)],
-        6: [lambda: x_ring1(6, out_h, False)],
-        7: [mix_grad],
+        7: [mix_grad, lambda: x_ring1(6, out_h, False)],
         8: [lambda: heads(0, 3)],
-        9: [lambda: heads(3, 6), head_end],
-        10: [input_grad, lambda: start(pair[:1]), lambda: x_ring2(6)],
-        11: [exchange_end, lambda: small_add(0), lambda: start(pair[1:2])],
-        12: [layer_end, lambda: small_add(1), lambda: start(pair[2:])],
-        13: [input_end, lambda: small_add(2), lambda: start(quad_y)],
-        14: [lambda: small_quad(quad_y, 3, y), lambda: start(quad_z)],
-        15: [lambda: small_quad(quad_z, 7, z)],
+        9: [lambda: heads(3, 6), head_end, lambda: x_ring2(6)],
+        10: [exchange_end],
+        11: [input_grad],
+        12: [small_add, lambda: start(quad_y)],
+        13: [layer_end],
+        14: [input_end, lambda: small_quad(quad_y, 1, y), lambda: start(quad_z)],
+        16: [lambda: small_quad(quad_z, 5, z), lambda: start(quad_x)],
     }
 
     load(jnp.int32(0), lambda copy: copy.start())
@@ -662,38 +677,25 @@
     grads(jnp.int32(0))
 
     def tick(n, _):
-        @pl.when((n >= R_SLOTS) & (n <= NU + 4))
+        @pl.when((n >= R_SLOTS) & (n <= NU + 2))
         def _():
             for i in range(4):
                 pl.semaphore_wait(credit.at[i], 1)
 
         @pl.when(n < NU)
         def _():
-            for j in range(4):
-                step_copy(n, 1, j).start()
-
-        for s in range(1, 7):
+            for j in range(2):
+                for way in range(2):
+                    step_copy(n, 1, j, way).start()
+
+        for s in range(1, 5):
             u = n - s
-            stage, m = (0, s) if s <= 3 else (1, s - 3)
 
             @pl.when((u >= 0) & (u < NU))
             def _():
-                g, r = lax.rem(u, G_SLOTS), lax.rem(u, R_SLOTS)
-                for j in range(4):
-                    copy = step_copy(u, s, j)
-                    copy.wait_recv()
-                    _, p, d = way(j, stage)
-                    at = chunk(g, j, stage, lax.rem(p - d * (m + 1) + 8, 4))
-                    at[...] = at[...] + (R2 if stage else R1)[r, m - 1, j]
-                    if s < 6:
-                        step_copy(u, s + 1, j).start()
-                    copy.wait_send()
-                if s == 6:
-                    for i in range(1, 4):
-                        last_copy(u, i).start()
-                    F[me, u] = G[g, y, xh, z, c]
-
-        @pl.when((n >= 1) & (n <= NU + 5 - R_SLOTS))
+                advance(u, s)
+
+        @pl.when((n >= 1) & (n <= NU + 3 - R_SLOTS))
         def _():
             for i, to in enumerate((ring["y"][1], ring["y"][0], ring["z"][1], ring["z"][0])):
                 pl.semaphore_signal(credit.at[i], inc=1, device_id=to, device_id_type=MESH)
@@ -718,6 +720,7 @@
     di_copy.wait()
     din_o[mine, :] = dn1[mine, :].astype(BF)
     din_o[other, :] = dir[...].astype(BF)
+    small_quad(quad_x, 9, me)
     small_o[...] = small[...]
 
     def finish(u, _):
@@ -767,20 +770,20 @@
         out_specs=(whole,) * 10,
         scratch_shapes=[
             VM((4, NU, 24, UW), F32),
-            VM((G_SLOTS, 4, 2, 4, 2, 24, UW), F32),
-            VM((R_SLOTS, 3, 4, 4, 24, UW), F32),
-            VM((R_SLOTS, 3, 4, 24, UW), F32),
+            VM((G_SLOTS, 2, 4, 2, 4, 24, UW), F32),
+            VM((R_SLOTS, 2, 2, 4, 24, UW), F32), VM((R_SLOTS, 2, 2, 2, 4, 24, UW), F32),
+            VM((R_SLOTS, 2, 2, 24, UW), F32), VM((R_SLOTS, 2, 2, 2, 24, UW), F32),
             VM((2, 4 * TOK, UW), BF),
-            VM((2, TOK, D), F32), VM((2, TOK, D), F32),
+            VM((4, HALF, D), F32), VM((4, HALF, D), F32),
             VM((2, HALF // 2, D), F32), VM((2, HALF, D), F32),
             VM((TOK, D), F32), VM((TOK, D), F32), VM((HALF, D), F32), VM((D, 2 * TOK), BF),
             VM((TOK, QW), BF), VM((TOK, QW), F32), VM((TOK, QW), F32), VM((2 * TOK, QW), BF),
             VM((2, TOK, WIDTH), F32), VM((2, TOK, WIDTH), F32), VM((2 * TOK, WIDTH), BF),
             VM((TOK, D), F32), VM((HALF, D), F32), VM((HALF, D), F32), VM((TOK, D), F32),
-            VM((8, D), F32), VM((11, 8, D), F32),
-            dma((R_SLOTS, 6, 4)), dma((R_SLOTS, 6, 4)), dma((NU, 3)), dma((NU, 3)),
-            regular((4,)), dma((19,)), dma((19,)), regular((3,)), dma((2,)), dma((2,)),
-            dma((9,)), dma((9,)),
+            VM((8, D), F32), VM((13, 8, D), F32),
+            dma((R_SLOTS, 4, 2, 2)), dma((R_SLOTS, 4, 2, 2)), dma((NU, 3)), dma((NU, 3)),
+            regular((4,)), dma((19,)), dma((19,)), regular((3,)), dma((1,)), dma((2,)),
+            dma((10,)), dma((10,)),
         ],
         compiler_params=pltpu.CompilerParams(
             collective_id=2, has_side_effects=True, vmem_limit_bytes=63 * 2**20
@@ -792,19 +795,12 @@
     tokens, lengths, keep_mask, norm1_gain, w_query, b_query, w_key, b_key, w_value, b_value,
     w_out, norm2_gain, w_gate, w_up, w_down, cotangent,
 ):
-    inv_freq = ROPE_BASE ** (-jnp.arange(0, WIDTH, 2).astype(F32) / WIDTH)
-    inv_freq = jnp.concatenate([inv_freq, inv_freq])[None, :]
-    g1 = norm1_gain.astype(F32)[None, :]
-    g2 = norm2_gain.astype(F32)[None, :]
-
-    def bias(b):
-        return b.astype(F32).reshape(1, -1)
-
-    q, k, v, mask, cos, sin, h1, n2, n2t, dy, dyt, la, o2 = front(
-        tokens, cotangent, lengths, keep_mask[None, :], inv_freq, g1, w_query, bias(b_query),
-        w_key, bias(b_key), w_value, bias(b_value), w_out, g2,
+    g1 = norm1_gain[None, :]
+    g2 = norm2_gain[None, :]
+    q, k, v, mask, cos, sin, h1, la, o2, n2t, dyt, dgu, a, dn2_part, out_part = front(
+        tokens, cotangent, lengths, keep_mask[None, :], g1, w_query, b_query, w_key, b_key,
+        w_value, b_value, w_out, g2, w_gate, w_up, w_down,
     )
-    dgu, a, dn2_part, out_part = ffn(n2, dy, w_gate, w_up, w_down)
     gate, up, down, dq, dk, dv, dout, layer_out, d_input, small = back(
         n2t, dyt, dgu, a, dn2_part, out_part, la, o2, tokens, cotangent, h1, q, k, v, mask, cos, sin,
         g1, g2, w_query, w_key, w_value, w_out,

time: 348 us -> 289 us (0.83)
  Pallas kernels: 327 us -> 264 us
  local copies, waits for them, and re-layouts: 16 us -> 20.6 us
  other arithmetic: 3.62 us -> 0 us
    pallas_call x1 -> x0, Pallas kernels: 38 us -> none  [ffn(): pl.pallas_call(ffn_kernel, name='ffn', out_shape=(shape((4 * TOK, 2 * FFW...]
    pallas_call x1, Pallas kernels: 205 us -> 173 us  [back(): pl.pallas_call(back_kernel, name='back', out_shape=(shape((24, FFL), F32)...]
    pallas_call x1, Pallas kernels: 84 us -> 90.6 us  [front(): pl.pallas_call(front_kernel, name='front', out_shape=(shape((TOK, QW), BF...]
    unnamed x24 -> x11, local copies, waits for them, and re-layouts: 9.48 us -> 14.1 us
where the time goes in v2:
time: 289 us; the launch traced here: 286 us
  Pallas kernels  264 us (91%)
  local copies, waits for them, and re-layouts  20.6 us (7%)
    pallas_call x1, Pallas kernels, back(): pl.pallas_call(back_kernel, name='back', out_shape=(shape((24, FFL), F32)...  173 us
    pallas_call x1, Pallas kernels, front(): pl.pallas_call(front_kernel, name='front', out_shape=(shape((TOK, QW), BF...  90.6 us
    unnamed x11, local copies, waits for them, and re-layouts  14.1 us

profile of v2, /device:TPU:1, one launch (start us, length us, event | category | flops | bytes accessed | tf_op | source)
XLA Modules:
  0.0 285.7 jit_solution(10455636571531145453)
XLA Ops:
  0.6 1.3 broadcast_in_dim.12.g1
  1.9 1.3 broadcast_in_dim.13.g2
  3.2 90.6 %front.1 = (bf16[256,768]{1,0:T(8,128)(2,1)}, bf16[256,128]{1,0:T(8,128)(2,1)}, bf16[256,128]{1,0:T(8,128)(2,1)}, f32[256,256]{1,0:T(8,128)}, f32[256,128]{1,0:T...) custom-call(bf16[256,1536]{1,0:T(8,128)(2,1)} %tokens.3, ...), custom_call_target="tpu_custom_call" | custom-call | tf_op jit(solution)/shard_map/front/pallas_call | solution.py:301
  93.9 173.4 %back.1 = (f32[24,4480]{1,0:T(8,128)}, f32[24,4480]{1,0:T(8,128)}, f32[24,4480]{1,0:T(8,128)}, f32[24,768]{1,0:T(8,128)}, f32[24,128]{1,0:T(8,128)}, /*index=5*/...) custom-call(bf16[1536,1024]{1,0:T(8,128)(2,1)} %get-tuple-element.39, ...), custom_call_target="tpu_custom_call" | custom-call | tf_op jit(solution)/shard_map/back/pallas_call | solution.py:761
  267.2 0.0 copy-start
  267.2 0.8 constant_dynamic-slice_fusion
  268.1 0.5 slice_bitcast_fusion
  268.6 1.3 slice_reduce_fusion
  269.9 1.2 fusion
  271.1 2.1 copy.39
  273.2 2.1 copy.40
  275.3 1.5 copy.41
  276.8 1.3 copy.42
  278.1 1.3 copy.43
  279.4 1.5 copy.44
  280.9 1.8 copy.45
  282.7 1.8 copy.46
  284.5 0.0 copy-done
  284.5 0.8 copy.47
Async XLA Ops:
  267.2 17.3 %copy-start = (f32[24,4480]{1,0:T(8,128)S(1)}, f32[24,4480]{1,0:T(8,128)}, u32[]{:S(2)}) copy-start(f32[24,4480]{1,0:T(8,128)} %get-tuple-element.63) | copy-start | bytes 1290244

commit v3 on v2

--- a/solution.py
+++ b/solution.py
@@ -18,6 +18,7 @@
 D = 1536
 TOK = 256
 HALF = 128
+SUB = 64
 HEADS = 6
 WIDTH = 128
 QW = HEADS * WIDTH
@@ -85,11 +86,11 @@
 
 
 def front_kernel(
-    tokens, cot, lengths, keep, g1, wq, bq, wk, bk, wv, bv, wo, g2, wg_h, wu_h, wd_h,
-    q_o, k_o, v_o, mask_o, cos_o, sin_o, h1_o, la_o, o2_o,
-    n2t_h, dyt_h, dgu_h, a_h, dn2_h, out_h,
-    n2f, dyf, n1f, n1r, of, orr, part, prec, wg, wu, wd, n2t_s, dyt_s, dgu_s, a_s, dn2_s, out_s,
-    ss, rs, wsem, osem, tsem,
+    lengths, keep, g1, bq, bk, bv, g2, tokens_h, cot_h, wq_h, wk_h, wv_h, wo_h, wg_h, wu_h, wd_h,
+    q_h, k_h, v_h, mask_h, cos_h, sin_h, h1_h, la_h, o2_h, n2t_h, dyt_h, dgu_h, a_h, dn2_h, out_h,
+    tokens, cot, wq, wk, wv, wo, wg, wu, wd, q_o, k_o, v_o, mask_o, cos_o, sin_o, h1_o, la_o, o2_o,
+    n2f, dyf, n1f, n1r, of, orr, part, prec, n2t_s, dyt_s, dgu_s, a_s, dn2_s, out_s,
+    ss, rs, isem, ksem, osem, psem, tsem,
 ):
     y, xh, z, c, t = coords()
     x = 2 * xh + t
@@ -99,30 +100,42 @@
     core = device(y, xh, z, 1 - c, t)
     mate = device(y, xh, z, c, 1 - t)
     cross = device_x(y, 3 - x, z, c)
+    me = 2 * xh + c
+    hidden = pl.ds(pl.multiple_of((me * 9 - me // 3) * 128, 128), FFW)
+    fetches = [
+        pltpu.make_async_copy(src, dst, isem.at[i])
+        for i, (src, dst) in enumerate((
+            (cot_h, cot), (tokens_h, tokens), (wk_h, wk), (wv_h, wv), (wq_h, wq), (wo_h, wo),
+            (wg_h.at[:, hidden], wg), (wu_h.at[:, hidden], wu), (wd_h.at[hidden, :], wd),
+        ))
+    ]
+    for copy in fetches[:6]:
+        copy.start()
     greet((right, left, core))
     mine = pl.ds(pl.multiple_of(t * HALF, HALF), HALF)
     other = pl.ds(pl.multiple_of((1 - t) * HALF, HALF), HALF)
-
-    def send(i, src, dst, to):
+    sent = []
+
+    def send(src, dst, to):
+        i = len(sent)
         copy = remote(src, dst, ss.at[i], rs.at[i], to)
         copy.start()
+        sent.append(copy)
         return copy
 
+    kept = []
+
+    def keep_copy(src, dst):
+        copy = pltpu.make_async_copy(src, dst, ksem.at[len(kept)])
+        copy.start()
+        kept.append(copy)
+
     near = pl.ds(2 * xh, 2)
-    far = pl.ds(2 * (1 - xh), 2)
+    fetches[0].wait()
     dyf[near, c] = cot[...].astype(F32).reshape(2, HALF, D)
-    dy_cross = send(0, dyf.at[near, c], dyf.at[near, c], cross)
-    dy_core = send(1, dyf.at[near, c], dyf.at[near, c], core)
-
-    me = 2 * xh + c
-    hidden = pl.ds(pl.multiple_of((me * 9 - me // 3) * 128, 128), FFW)
-    loads = [
-        pltpu.make_async_copy(wg_h.at[:, hidden], wg, wsem.at[0]),
-        pltpu.make_async_copy(wu_h.at[:, hidden], wu, wsem.at[1]),
-        pltpu.make_async_copy(wd_h.at[hidden, :], wd, wsem.at[2]),
-    ]
-    for copy in loads:
-        copy.start()
+    dy_own = send(dyf.at[x, c], dyf.at[x, c], cross)
+    x_mate = 2 * xh + 1 - t
+    dy_core = send(dyf.at[near, c], dyf.at[near, c], core)
 
     rows = lax.broadcasted_iota(jnp.int32, (TOK, TOK), 0)
     cols = lax.broadcasted_iota(jnp.int32, (TOK, TOK), 1)
@@ -137,7 +150,7 @@
         seg_r = seg_r + (rows >= end).astype(jnp.int32)
         seg_c = seg_c + (cols >= end).astype(jnp.int32)
         place = place - jnp.where(row_id >= end, span, 0)
-    allowed = (seg_r == seg_c) & (cols <= rows) & ((keep[...] == 1) | (cols == rows))
+    allowed = (seg_r == seg_c) & (cols <= rows) & ((keep[...][None, :] == 1) | (cols == rows))
     mask_o[...] = allowed.astype(F32)
     lane = lax.broadcasted_iota(jnp.int32, (TOK, WIDTH), 1)
     first = lane < WIDTH // 2
@@ -148,11 +161,16 @@
     cos_o[...] = cosine
     sin_o[...] = sine
 
+    fetches[1].wait()
     xf = tokens[...].astype(F32)
     r1 = lax.rsqrt(mean_last(xf * xf) + EPS)
-    n1 = (xf * r1 * g1[...].astype(F32)).astype(BF)
+    n1 = (xf * r1 * g1[...].astype(F32)[None, :]).astype(BF)
     n1f[...] = n1.astype(F32)
-    n1_core = send(2, n1f, n1r, core)
+    n1_core = send(n1f, n1r, core)
+    for copy in fetches[2:6]:
+        copy.wait()
+    for copy in fetches[6:]:
+        copy.start()
     kp = dot(n1, wk[...]) + bk[...].astype(F32)
     k_o[...] = rope(kp, cosine, sine).astype(BF)
     v_o[...] = (dot(n1, wv[...]) + bv[...].astype(F32)).astype(BF)
@@ -173,122 +191,164 @@
         return 0
 
     lax.fori_loop(0, HEADS, head, 0)
+
+    def quarter(n):
+        return pl.ds(n * SUB, SUB)
+
     part[0] = dot(o2_o[other, :], wo[...])
-    half = send(3, part.at[0], prec, mate)
-    o_core = send(4, of, orr, core)
+    halves = [send(part.at[0, quarter(n)], prec.at[quarter(n)], mate) for n in range(2)]
+    o_core = send(of, orr, core)
     part[1] = dot(o2_o[mine, :], wo[...])
+
+    order = (
+        ((x, 0, HALF),),
+        ((x3, 0, SUB), (x1, 0, SUB)),
+        ((x3, SUB, SUB), (x1, SUB, SUB)),
+        ((x2, 0, HALF),),
+    )
+
+    def pieces(n):
+        out, at = [], 0
+        for xx, lo, size in order[n]:
+            for cc in range(2):
+                out.append((at, size, xx, cc, lo))
+                at += size
+        return out
+
+    def gather(ref, n):
+        if len(order[n]) == 1:
+            return ref[order[n][0][0]].reshape(TOK, D).astype(BF)
+        return jnp.concatenate([ref[xx, cc, lo : lo + size] for _, size, xx, cc, lo in pieces(n)], axis=0).astype(BF)
+
+    def turned(n):
+        return pltpu.make_async_copy(dyt_s.at[n % 2], dyt_h.at[:, pl.ds(n * TOK, TOK)], tsem.at[n % 2])
+
+    def turn(n):
+        if n >= 2:
+            turned(n - 2).wait()
+        dyt_s[n % 2] = gather(dyf, n).T
+        turned(n).start()
+
+    for src, dst in ((q_o, q_h), (k_o, k_h), (v_o, v_h), (mask_o, mask_h), (cos_o, cos_h), (sin_o, sin_h)):
+        keep_copy(src, dst)
     la_o[:, :TOK] = n1.T
     n1_core.wait_recv()
     la_o[:, TOK:] = n1r[...].astype(BF).T
+    keep_copy(la_o, la_h)
     o_core.wait_recv()
     o2_o[TOK:, :] = orr[...].astype(BF)
-
-    half.wait_recv()
-    h1 = tokens[mine, :].astype(F32) + part[1] + prec[...]
-    h1_o[...] = h1
-    r2 = lax.rsqrt(mean_last(h1 * h1) + EPS)
-    n2f[x, c] = (h1 * r2 * g2[...].astype(F32)).astype(BF).astype(F32)
-
-    def pass_on(i, xx, to, lo=0, n=HALF):
-        at = n2f.at[xx, c, pl.ds(lo, n)]
-        return send(i, at, at, to)
-
-    to_right = pass_on(5, x, right)
-    to_left = pass_on(6, x, left)
-    to_core = pass_on(7, x, core)
+    keep_copy(o2_o, o2_h)
+    dy_core.wait_recv()
+    turn(0)
+
+    def pass_on(xx, to, lo, size):
+        at = n2f.at[xx, c, pl.ds(lo, size)]
+        return send(at, at, to)
+
+    to_right, to_left, to_core = [], [], []
+    for n in range(2):
+        halves[n].wait_recv()
+        at = quarter(n)
+        own = tokens[pl.ds(pl.multiple_of(t * HALF + n * SUB, SUB), SUB), :].astype(F32)
+        h1 = own + part[1, at] + prec[at]
+        h1_o[at] = h1
+        r2 = lax.rsqrt(mean_last(h1 * h1) + EPS)
+        n2f[x, c, at] = (h1 * r2 * g2[...].astype(F32)[None, :]).astype(BF).astype(F32)
+        to_right.append(pass_on(x, right, n * SUB, SUB))
+        to_left.append(pass_on(x, left, n * SUB, SUB))
+        to_core.append(pass_on(x, core, n * SUB, SUB))
+    keep_copy(h1_o, h1_h)
 
     unit = lax.broadcasted_iota(jnp.int32, (1, FFW), 1)
     live = jnp.where((unit < 128) & (me == 3), 0.0, 1.0)
 
-    def tokens_of(xx):
-        return pl.ds(pl.multiple_of(xx * TOK, TOK), TOK)
-
-    def results(n, xx):
-        slot, at = n % 2, tokens_of(xx)
-        return [
-            pltpu.make_async_copy(src, dst, osem.at[slot, i])
-            for i, (src, dst) in enumerate((
-                (n2t_s.at[slot], n2t_h.at[:, at]),
-                (dgu_s.at[slot], dgu_h.at[at]),
-                (a_s.at[slot], a_h.at[at]),
-                (dn2_s.at[slot], dn2_h.at[xx]),
-                (out_s.at[slot], out_h.at[xx]),
-            ))
-        ]
-
-    order = (x, x3, x1, x2)
+    def results(n):
+        slot, at = n % 2, pl.ds(n * TOK, TOK)
+        moves = [(n2t_s.at[slot], n2t_h.at[:, at]), (dgu_s.at[slot], dgu_h.at[at]), (a_s.at[slot], a_h.at[at])]
+        copies = [pltpu.make_async_copy(src, dst, osem.at[slot, i]) for i, (src, dst) in enumerate(moves)]
+        for b, (staged, dst) in enumerate(((dn2_s, dn2_h), (out_s, out_h))):
+            for i, (row, size, xx, cc, lo) in enumerate(pieces(n)):
+                copies.append(
+                    pltpu.make_async_copy(
+                        staged.at[slot, pl.ds(row, size)], dst.at[xx, cc, pl.ds(lo, size)], psem.at[slot, b, i]
+                    )
+                )
+        return copies
 
     def feed(n):
-        xx, slot = order[n], n % 2
-        if n >= 2:
-            for copy in results(n - 2, order[n - 2]):
-                copy.wait()
-        here = n2f[xx].reshape(TOK, D).astype(BF)
+        slot = n % 2
+        here = gather(n2f, n)
         g = dot(here, wg[...])
         u = dot(here, wu[...])
+        if n >= 2:
+            for copy in results(n - 2):
+                copy.wait()
         n2t_s[slot] = here.T
         sg = live / (1.0 + jnp.exp(-g))
         silu = g * sg
         a = (silu * u).astype(BF)
         a_s[slot] = a
-        out_s[slot] = dot(a, wd[...]).reshape(2, HALF, D)
-        da = dot_nt(dyf[xx].reshape(TOK, D).astype(BF), wd[...])
+        out_s[slot] = dot(a, wd[...])
+        da = dot_nt(gather(dyf, n), wd[...])
         dg = (da * u * sg * (1.0 + g * (1.0 - sg))).astype(BF)
         du = (da * silu).astype(BF)
         dgu_s[slot, :, :FFW] = dg
         dgu_s[slot, :, FFW:] = du
-        dn2_s[slot] = (dot_nt(dg, wg[...]) + dot_nt(du, wu[...])).reshape(2, HALF, D)
-        for copy in results(n, xx):
+        dn2_s[slot] = dot_nt(dg, wg[...]) + dot_nt(du, wu[...])
+        for copy in results(n):
             copy.start()
 
-    def turned(n, xx):
-        return pltpu.make_async_copy(dyt_s.at[n % 2], dyt_h.at[:, tokens_of(xx)], tsem.at[n % 2])
-
-    around = (x, 2 * xh + 1 - t, x2, 3 - x)
-
-    def turn(n):
-        xx = around[n]
-        if n >= 2:
-            turned(n - 2, around[n - 2]).wait()
-        dyt_s[n % 2] = dyf[xx].reshape(TOK, D).astype(BF).T
-        turned(n, xx).start()
-
-    dy_core.wait_recv()
-    to_core.wait_recv()
-    for copy in loads:
+    passed, core_side, core_across = [], [], []
+
+    dy_mate = send(dyf.at[x_mate, c], dyf.at[x_mate, c], cross)
+
+    def step_one(n):
+        to_right[n].wait_recv()
+        passed.append(pass_on(x3, right, n * SUB, SUB // 2))
+        core_side.append(pass_on(x3, core, n * SUB, SUB))
+        to_left[n].wait_recv()
+        passed.append(pass_on(x1, left, n * SUB + SUB // 2, SUB // 2))
+        core_side.append(pass_on(x1, core, n * SUB, SUB))
+
+    def step_two(n):
+        for copy in passed[2 * n : 2 * n + 2]:
+            copy.wait_recv()
+        core_across.append(pass_on(x2, core, n * SUB, SUB))
+
+    for copy in to_core:
+        copy.wait_recv()
+    for copy in fetches[6:]:
         copy.wait()
     feed(0)
-    turn(0)
+    step_one(0)
+    dy_own.wait_recv()
+    dy_side = send(dyf.at[3 - x, c], dyf.at[3 - x, c], core)
+    dy_side.wait_recv()
     turn(1)
-    dy_cross.wait_recv()
-    dy_far = send(8, dyf.at[far, c], dyf.at[far, c], core)
-
-    to_right.wait_recv()
-    pass_right = pass_on(9, x3, right, 0, HALF // 2)
-    core_left = pass_on(10, x3, core)
-    to_left.wait_recv()
-    pass_left = pass_on(11, x1, left, HALF // 2, HALF // 2)
-    core_right = pass_on(12, x1, core)
-    dy_far.wait_recv()
-    core_left.wait_recv()
+    for copy in core_side:
+        copy.wait_recv()
     feed(1)
-    pass_right.wait_recv()
-    pass_left.wait_recv()
-    core_across = pass_on(13, x2, core)
-    core_right.wait_recv()
+    step_one(1)
+    turn(2)
+    for copy in core_side[2:]:
+        copy.wait_recv()
     feed(2)
-    turn(2)
+    step_two(0)
+    dy_mate.wait_recv()
+    dy_across = send(dyf.at[x2, c], dyf.at[x2, c], core)
+    step_two(1)
+    dy_across.wait_recv()
     turn(3)
-    core_across.wait_recv()
+    for copy in core_across:
+        copy.wait_recv()
     feed(3)
     for n in (2, 3):
-        turned(n, around[n]).wait()
-        for copy in results(n, order[n]):
+        turned(n).wait()
+        for copy in results(n):
             copy.wait()
-    for copy in (
-        dy_cross, dy_core, n1_core, half, o_core, to_right, to_left, to_core,
-        dy_far, pass_right, core_left, pass_left, core_right, core_across,
-    ):
+    for copy in kept:
+        copy.wait()
+    for copy in sent:
         copy.wait_send()
 
 
@@ -309,18 +369,23 @@
             shape((4 * TOK, 2 * FFW), BF), shape((4 * TOK, FFW), BF),
             shape((4, 2, HALF, D), F32), shape((4, 2, HALF, D), F32),
         ),
-        in_specs=[whole, whole, scalars] + [whole] * 10 + [hbm] * 3,
-        out_specs=(whole,) * 9 + (hbm,) * 6,
+        in_specs=[scalars] + [whole] * 6 + [hbm] * 9,
+        out_specs=(hbm,) * 15,
         scratch_shapes=[
+            VM((TOK, D), BF), VM((TOK, D), BF),
+            VM((D, QW), BF), VM((D, WIDTH), BF), VM((D, WIDTH), BF), VM((QW, D), BF),
+            VM((D, FFW), BF), VM((D, FFW), BF), VM((FFW, D), BF),
+            VM((TOK, QW), BF), VM((TOK, WIDTH), BF), VM((TOK, WIDTH), BF),
+            VM((TOK, TOK), F32), VM((TOK, WIDTH), F32), VM((TOK, WIDTH), F32),
+            VM((HALF, D), F32), VM((D, 2 * TOK), BF), VM((2 * TOK, QW), BF),
             VM((4, 2, HALF, D), F32), VM((4, 2, HALF, D), F32),
             VM((TOK, D), F32), VM((TOK, D), F32),
             VM((TOK, QW), F32), VM((TOK, QW), F32),
             VM((2, HALF, D), F32), VM((HALF, D), F32),
-            VM((D, FFW), BF), VM((D, FFW), BF), VM((FFW, D), BF),
             VM((2, D, TOK), BF), VM((2, D, TOK), BF),
             VM((2, TOK, 2 * FFW), BF), VM((2, TOK, FFW), BF),
-            VM((2, 2, HALF, D), F32), VM((2, 2, HALF, D), F32),
-            dma((14,)), dma((14,)), dma((3,)), dma((2, 5)), dma((2,)),
+            VM((2, TOK, D), F32), VM((2, TOK, D), F32),
+            dma((32,)), dma((32,)), dma((9,)), dma((9,)), dma((2, 3)), dma((2, 2, 4)), dma((2,)),
         ],
         compiler_params=pltpu.CompilerParams(
             collective_id=1, has_side_effects=True, vmem_limit_bytes=63 * 2**20
@@ -329,13 +394,24 @@
 
 
 def back_kernel(
-    n2t, dyt, dgu_h, a_h, dn2_h, out_h, la, o2, tokens, cot, h1, q, k, v, mask, cos, sin,
-    g1, g2, wq, wk, wv, wo,
-    gate_o, up_o, down_o, dq_o, dk_o, dv_o, dout_o, lout_o, din_o, small_o,
+    dgu_h, a_h, dn2_h, out_h, g1, g2, n2t_h, dyt_h, la_h, o2_h, tokens_h, cot_h, h1_h, q_h, k_h, v_h,
+    mask_h, cos_h, sin_h, wq_h, wk_h, wv_h, wo_h,
+    F_o, lout_o, din_o, small_o,
+    n2t, dyt, la, o2, tokens, cot, h1, q, k, v, mask, cos, sin, wq, wk, wv, wo,
     F, G, R1, R2, R3, R4, RB, C, L, S1, S2, dhf, dhr, dh, lb, do, dqf, xqr, rq, dkvf, xkvr, rkv,
     dn1, dn1r, dir, lof, small, sb,
-    ss, rs, fss, frs, credit, xss, xrs, free, lsem, bsem, sss, srs,
+    ss, rs, fss, frs, credit, xss, xrs, free, lsem, bsem, sss, srs, isem,
 ):
+    fetches = [
+        pltpu.make_async_copy(src, dst, isem.at[i])
+        for i, (src, dst) in enumerate((
+            (n2t_h, n2t), (dyt_h, dyt), (cot_h, cot), (h1_h, h1), (wo_h, wo), (q_h, q), (k_h, k), (v_h, v),
+            (mask_h, mask), (cos_h, cos), (sin_h, sin), (tokens_h, tokens), (wq_h, wq), (wk_h, wk),
+            (wv_h, wv), (la_h, la), (o2_h, o2),
+        ))
+    ]
+    for copy in fetches[:1]:
+        copy.start()
     y, xh, z, c, t = coords()
     x = 2 * xh + t
     me = 2 * xh + c
@@ -547,7 +623,7 @@
         hh = h1[...]
         r2 = lax.rsqrt(mean_last(hh * hh) + EPS)
         normed = hh * r2
-        e = dn2 * g2[...].astype(F32)
+        e = dn2 * g2[...].astype(F32)[None, :]
         grad = cot[mine, :].astype(F32) + r2 * (e - normed * mean_last(e * normed))
         dh[...] = grad
         dhf[mine, :] = grad.astype(BF).astype(F32)
@@ -628,7 +704,7 @@
         xf = tokens[mine, :].astype(F32)
         r1 = lax.rsqrt(mean_last(xf * xf) + EPS)
         normed = xf * r1
-        e = total * g1[...].astype(F32)
+        e = total * g1[...].astype(F32)[None, :]
         grad = dh[...] + r1 * (e - normed * mean_last(e * normed))
         dn1[mine, :] = grad.astype(BF).astype(F32)
         di_copy.start()
@@ -656,9 +732,13 @@
         for copy in copies:
             copy.start()
 
+    def fetched():
+        for copy in fetches[1:]:
+            copy.wait()
+
     extras = {
         0: [lambda: x_begin(0, dn2_h, True)],
-        1: [lambda: x_ring1(0, dn2_h, True)],
+        1: [lambda: x_ring1(0, dn2_h, True), fetched],
         3: [lambda: x_ring2(0)],
         5: [second_norm, lambda: x_begin(6, out_h, False)],
         7: [mix_grad, lambda: x_ring1(6, out_h, False)],
@@ -674,6 +754,8 @@
 
     load(jnp.int32(0), lambda copy: copy.start())
     load(jnp.int32(1), lambda copy: copy.start())
+    start(fetches[1:])
+    fetches[0].wait()
     grads(jnp.int32(0))
 
     def tick(n, _):
@@ -734,6 +816,14 @@
         return 0
 
     lax.fori_loop(0, NU, finish, 0)
+    F_o[...] = F[...]
+
+
+def finish_kernel(
+    F, lout, din, small, lout_o, din_o, n1_o, dq_o, bq_o, dk_o, bk_o, dv_o, bv_o, dout_o, n2_o, gate_o, up_o, down_o
+):
+    lout_o[...] = lout[...]
+    din_o[...] = din[...]
 
     def tile(i, col):
         return F[i, col // UW, :, col % UW : col % UW + 128]
@@ -741,7 +831,8 @@
     for m, out in enumerate((gate_o, up_o, down_o)):
         for i in range(4):
             for n in range(1 if i == 3 else 0, 9):
-                out[:, OFFS[i] + 128 * n : OFFS[i] + 128 * (n + 1)] = tile(i, m * FFW + 128 * n)
+                at = slice(OFFS[i] + 128 * n, OFFS[i] + 128 * (n + 1))
+                out[:, at] = tile(i, m * FFW + 128 * n)
     base = 3 * FFW
     dk_o[...] = tile(0, base) + tile(2, base)
     dv_o[...] = tile(1, base) + tile(3, base)
@@ -750,6 +841,32 @@
         col = base + 128 * (n + 1)
         dq_o[:, at] = tile(0, col) + tile(2, col)
         dout_o[:, at] = tile(1, col) + tile(3, col)
+        bq_o[n : n + 1, :] = small[2:3, at]
+    bk_o[...] = small[2:3, QW : QW + WIDTH]
+    bv_o[...] = small[2:3, QW + WIDTH : QW + 2 * WIDTH]
+    lane = lax.broadcasted_iota(jnp.int32, (24, D), 1)
+    row = lax.broadcasted_iota(jnp.int32, (24, D), 0)
+    own = lane == row + lax.axis_index("dp") * 24
+    n2_o[...] = jnp.sum(jnp.where(own, small[0:1, :], 0.0), axis=1)
+    n1_o[...] = jnp.sum(jnp.where(own, small[1:2, :], 0.0), axis=1)
+
+
+def finish(*args):
+    shape = jax.ShapeDtypeStruct
+    whole = pl.BlockSpec(memory_space=VM)
+    return pl.pallas_call(
+        finish_kernel,
+        name="finish",
+        out_shape=(
+            shape((TOK, D), BF), shape((TOK, D), BF), shape((24,), F32), shape((24, QW), F32),
+            shape((HEADS, WIDTH), F32), shape((24, WIDTH), F32), shape((1, WIDTH), F32),
+            shape((24, WIDTH), F32), shape((1, WIDTH), F32), shape((24, QW), F32), shape((24,), F32),
+            shape((24, FFL), F32), shape((24, FFL), F32), shape((24, FFL), F32),
+        ),
+        in_specs=[whole] * 4,
+        out_specs=(whole,) * 14,
+        compiler_params=pltpu.CompilerParams(vmem_limit_bytes=60 * 2**20),
+    )(*args)
 
 
 def back(*args):
@@ -762,13 +879,16 @@
         back_kernel,
         name="back",
         out_shape=(
-            shape((24, FFL), F32), shape((24, FFL), F32), shape((24, FFL), F32),
-            shape((24, QW), F32), shape((24, WIDTH), F32), shape((24, WIDTH), F32), shape((24, QW), F32),
-            shape((TOK, D), BF), shape((TOK, D), BF), shape((8, D), F32),
+            shape((4, NU, 24, UW), F32), shape((TOK, D), BF), shape((TOK, D), BF), shape((8, D), F32),
         ),
-        in_specs=[whole, whole] + [hbm] * 4 + [whole] * 17,
-        out_specs=(whole,) * 10,
+        in_specs=[hbm] * 4 + [whole] * 2 + [hbm] * 17,
+        out_specs=(whole,) * 4,
         scratch_shapes=[
+            VM((D, 4 * TOK), BF), VM((D, 4 * TOK), BF), VM((D, 2 * TOK), BF), VM((2 * TOK, QW), BF),
+            VM((TOK, D), BF), VM((TOK, D), BF), VM((HALF, D), F32),
+            VM((TOK, QW), BF), VM((TOK, WIDTH), BF), VM((TOK, WIDTH), BF),
+            VM((TOK, TOK), F32), VM((TOK, WIDTH), F32), VM((TOK, WIDTH), F32),
+            VM((D, QW), BF), VM((D, WIDTH), BF), VM((D, WIDTH), BF), VM((QW, D), BF),
             VM((4, NU, 24, UW), F32),
             VM((G_SLOTS, 2, 4, 2, 4, 24, UW), F32),
             VM((R_SLOTS, 2, 2, 4, 24, UW), F32), VM((R_SLOTS, 2, 2, 2, 4, 24, UW), F32),
@@ -783,7 +903,7 @@
             VM((8, D), F32), VM((13, 8, D), F32),
             dma((R_SLOTS, 4, 2, 2)), dma((R_SLOTS, 4, 2, 2)), dma((NU, 3)), dma((NU, 3)),
             regular((4,)), dma((19,)), dma((19,)), regular((3,)), dma((1,)), dma((2,)),
-            dma((10,)), dma((10,)),
+            dma((10,)), dma((10,)), dma((17,)),
         ],
         compiler_params=pltpu.CompilerParams(
             collective_id=2, has_side_effects=True, vmem_limit_bytes=63 * 2**20
@@ -795,34 +915,16 @@
     tokens, lengths, keep_mask, norm1_gain, w_query, b_query, w_key, b_key, w_value, b_value,
     w_out, norm2_gain, w_gate, w_up, w_down, cotangent,
 ):
-    g1 = norm1_gain[None, :]
-    g2 = norm2_gain[None, :]
     q, k, v, mask, cos, sin, h1, la, o2, n2t, dyt, dgu, a, dn2_part, out_part = front(
-        tokens, cotangent, lengths, keep_mask[None, :], g1, w_query, b_query, w_key, b_key,
-        w_value, b_value, w_out, g2, w_gate, w_up, w_down,
+        lengths, keep_mask, norm1_gain, b_query, b_key, b_value, norm2_gain,
+        tokens, cotangent, w_query, w_key, w_value, w_out, w_gate, w_up, w_down,
     )
-    gate, up, down, dq, dk, dv, dout, layer_out, d_input, small = back(
-        n2t, dyt, dgu, a, dn2_part, out_part, la, o2, tokens, cotangent, h1, q, k, v, mask, cos, sin,
-        g1, g2, w_query, w_key, w_value, w_out,
-    )
-    mine = lax.dynamic_slice(small, (0, lax.axis_index("dp") * 24), (8, 24))
-    biases = small[2]
-    return (
-        layer_out,
-        d_input,
-        mine[1],
-        dq,
-        biases[:QW].reshape(HEADS, WIDTH),
-        dk,
-        biases[QW : QW + WIDTH][None, :],
-        dv,
-        biases[QW + WIDTH : QW + 2 * WIDTH][None, :],
-        dout.T,
-        mine[0],
-        gate,
-        up,
-        down.T,
-    )
+    results = list(finish(*back(
+        dgu, a, dn2_part, out_part, norm1_gain, norm2_gain, n2t, dyt, la, o2, tokens, cotangent, h1,
+        q, k, v, mask, cos, sin, w_query, w_key, w_value, w_out,
+    )))
+    results[9], results[13] = results[9].T, results[13].T
+    return tuple(results)
 
 
 def solution(mesh):

time: 289 us -> 263 us (0.910)
  local copies, waits for them, and re-layouts: 20.6 us -> 0 us
  Pallas kernels: 264 us -> 259 us
    unnamed x11 -> x0, local copies, waits for them, and re-layouts: 14.1 us -> none
    pallas_call x1, Pallas kernels: 90.6 us -> 79 us  [front(): pl.pallas_call(front_kernel, name='front', out_shape=(shape((TOK, QW), BF...]
    pallas_call x1 -> x2, Pallas kernels: 173 us -> 180 us  [the longest x1 176 us: back(): pl.pallas_call(back_kernel, name='back', out_shape=(shape((4, NU, 24, UW)...]
where the time goes in v3:
time: 263 us; the launch traced here: 260 us
  Pallas kernels  259 us (98%)
    pallas_call x1, Pallas kernels, back(): pl.pallas_call(back_kernel, name='back', out_shape=(shape((4, NU, 24, UW)...  176 us
    pallas_call x1, Pallas kernels, front(): pl.pallas_call(front_kernel, name='front', out_shape=(shape((TOK, QW), BF...  79 us

profile of v3, /device:TPU:1, one launch (start us, length us, event | category | flops | bytes accessed | tf_op | source)
XLA Modules:
  0.0 260.0 jit_solution(11321309106592316758)
XLA Ops:
  0.6 79.0 %front.1 = (bf16[256,768]{1,0:T(8,128)(2,1)}, bf16[256,128]{1,0:T(8,128)(2,1)}, bf16[256,128]{1,0:T(8,128)(2,1)}, f32[256,256]{1,0:T(8,128)}, f32[256,128]{1,0:T...) custom-call(s32[1,4]{1,0:T(1,128)} %lengths.1, ...), custom_call_target="tpu_custom_call" | custom-call | tf_op jit(solution)/shard_map/front/pallas_call | solution.py:361
  79.7 176.2 %back.1 = (f32[4,17,24,256]{3,2,1,0:T(8,128)}, bf16[256,1536]{1,0:T(8,128)(2,1)}, bf16[256,1536]{1,0:T(8,128)(2,1)}, f32[8,1536]{1,0:T(8,128)}) custom-call(bf16[1024,2304]{1,0:T(8,128)(2,1)} %get-tuple-element.47.dgu_h, bf16[1024,1152]{1,0:T(8,128)(2,1)} %get-tuple-element.48.a_h, f32[4,2,128,1536]{3,2,1,0:T(8,128)} %get-tuple-element.49.dn2_h, ...), custom_call_target="tpu_custom_call" | custom-call | tf_op jit(solution)/shard_map/back/pallas_call | solution.py:878
  255.8 3.7 %finish.1 = (bf16[256,1536]{1,0:T(8,128)(2,1)}, bf16[256,1536]{1,0:T(8,128)(2,1)}, f32[24]{0:T(128)}, f32[24,768]{1,0:T(8,128)}, f32[6,128]{1,0:T(8,128)}, /*ind...) custom-call(f32[4,17,24,256]{3,2,1,0:T(8,128)} %get-tuple-element.62, ...), custom_call_target="tpu_custom_call" | custom-call | tf_op jit(solution)/shard_map/finish/pallas_call | solution.py:857

commit v4 on v3

--- a/solution.py
+++ b/solution.py
@@ -88,7 +88,7 @@
 def front_kernel(
     lengths, keep, g1, bq, bk, bv, g2, tokens_h, cot_h, wq_h, wk_h, wv_h, wo_h, wg_h, wu_h, wd_h,
     q_h, k_h, v_h, mask_h, cos_h, sin_h, h1_h, la_h, o2_h, n2t_h, dyt_h, dgu_h, a_h, dn2_h, out_h,
-    tokens, cot, wq, wk, wv, wo, wg, wu, wd, q_o, k_o, v_o, mask_o, cos_o, sin_o, h1_o, la_o, o2_o,
+    tokens, cot, wq, wk, wv, wo, wgu, wd, q_o, k_o, v_o, mask_o, cos_o, sin_o, h1_o, la_o, o2_o,
     n2f, dyf, n1f, n1r, of, orr, part, prec, n2t_s, dyt_s, dgu_s, a_s, dn2_s, out_s,
     ss, rs, isem, ksem, osem, psem, tsem,
 ):
@@ -106,7 +106,8 @@
         pltpu.make_async_copy(src, dst, isem.at[i])
         for i, (src, dst) in enumerate((
             (cot_h, cot), (tokens_h, tokens), (wk_h, wk), (wv_h, wv), (wq_h, wq), (wo_h, wo),
-            (wg_h.at[:, hidden], wg), (wu_h.at[:, hidden], wu), (wd_h.at[hidden, :], wd),
+            (wg_h.at[:, hidden], wgu.at[:, pl.ds(0, FFW)]), (wu_h.at[:, hidden], wgu.at[:, pl.ds(FFW, FFW)]),
+            (wd_h.at[hidden, :], wd),
         ))
     ]
     for copy in fetches[:6]:
@@ -273,15 +274,16 @@
                         staged.at[slot, pl.ds(row, size)], dst.at[xx, cc, pl.ds(lo, size)], psem.at[slot, b, i]
                     )
                 )
-        return copies
+        early = (0, 2) + tuple(range(3 + len(pieces(n)), len(copies)))
+        return [copies[i] for i in early], [copy for i, copy in enumerate(copies) if i not in early]
 
     def feed(n):
         slot = n % 2
         here = gather(n2f, n)
-        g = dot(here, wg[...])
-        u = dot(here, wu[...])
+        both = dot(here, wgu[...])
+        g, u = both[:, :FFW], both[:, FFW:]
         if n >= 2:
-            for copy in results(n - 2):
+            for copy in sum(results(n - 2), []):
                 copy.wait()
         n2t_s[slot] = here.T
         sg = live / (1.0 + jnp.exp(-g))
@@ -289,18 +291,23 @@
         a = (silu * u).astype(BF)
         a_s[slot] = a
         out_s[slot] = dot(a, wd[...])
+        early, late = results(n)
+        for copy in early:
+            copy.start()
         da = dot_nt(gather(dyf, n), wd[...])
         dg = (da * u * sg * (1.0 + g * (1.0 - sg))).astype(BF)
         du = (da * silu).astype(BF)
         dgu_s[slot, :, :FFW] = dg
         dgu_s[slot, :, FFW:] = du
-        dn2_s[slot] = dot_nt(dg, wg[...]) + dot_nt(du, wu[...])
-        for copy in results(n):
+        dn2_s[slot] = dot_nt(dgu_s[slot], wgu[...])
+        for copy in late:
             copy.start()
 
     passed, core_side, core_across = [], [], []
 
-    dy_mate = send(dyf.at[x_mate, c], dyf.at[x_mate, c], cross)
+    dy_mate = send(dyf.at[x_mate, c, pl.ds(0, 96)], dyf.at[x_mate, c, pl.ds(0, 96)], cross)
+    dy_own.wait_recv()
+    dy_pass = send(dyf.at[3 - x, c, pl.ds(96, 32)], dyf.at[3 - x, c, pl.ds(96, 32)], mate)
 
     def step_one(n):
         to_right[n].wait_recv()
@@ -321,7 +328,6 @@
         copy.wait()
     feed(0)
     step_one(0)
-    dy_own.wait_recv()
     dy_side = send(dyf.at[3 - x, c], dyf.at[3 - x, c], core)
     dy_side.wait_recv()
     turn(1)
@@ -335,6 +341,7 @@
     feed(2)
     step_two(0)
     dy_mate.wait_recv()
+    dy_pass.wait_recv()
     dy_across = send(dyf.at[x2, c], dyf.at[x2, c], core)
     step_two(1)
     dy_across.wait_recv()
@@ -344,7 +351,7 @@
     feed(3)
     for n in (2, 3):
         turned(n).wait()
-        for copy in results(n):
+        for copy in sum(results(n), []):
             copy.wait()
     for copy in kept:
         copy.wait()
@@ -374,7 +381,7 @@
         scratch_shapes=[
             VM((TOK, D), BF), VM((TOK, D), BF),
             VM((D, QW), BF), VM((D, WIDTH), BF), VM((D, WIDTH), BF), VM((QW, D), BF),
-            VM((D, FFW), BF), VM((D, FFW), BF), VM((FFW, D), BF),
+            VM((D, 2 * FFW), BF), VM((FFW, D), BF),
             VM((TOK, QW), BF), VM((TOK, WIDTH), BF), VM((TOK, WIDTH), BF),
             VM((TOK, TOK), F32), VM((TOK, WIDTH), F32), VM((TOK, WIDTH), F32),
             VM((HALF, D), F32), VM((D, 2 * TOK), BF), VM((2 * TOK, QW), BF),

time: 263 us -> 252 us (0.958); the launches traced: 260 us -> 252 us
  Pallas kernels: 259 us -> 251 us
    pallas_call x1, Pallas kernels: 79 us -> 73 us  [front(): pl.pallas_call(front_kernel, name='front', out_shape=(shape((TOK, QW), BF...]
where the time goes in v4:
time: 252 us
  Pallas kernels  251 us (100%)
    pallas_call x1, Pallas kernels, back(): pl.pallas_call(back_kernel, name='back', out_shape=(shape((4, NU, 24, UW)...  174 us
    pallas_call x1, Pallas kernels, front(): pl.pallas_call(front_kernel, name='front', out_shape=(shape((TOK, QW), BF...  73 us

profile of v4, /device:TPU:1, one launch (start us, length us, event | category | flops | bytes accessed | tf_op | source)
XLA Modules:
  0.0 251.7 jit_solution(17320409372762254832)
XLA Ops:
  0.6 73.0 %front.1 = (bf16[256,768]{1,0:T(8,128)(2,1)}, bf16[256,128]{1,0:T(8,128)(2,1)}, bf16[256,128]{1,0:T(8,128)(2,1)}, f32[256,256]{1,0:T(8,128)}, f32[256,128]{1,0:T...) custom-call(s32[1,4]{1,0:T(1,128)} %lengths.1, ...), custom_call_target="tpu_custom_call" | custom-call | tf_op jit(solution)/shard_map/front/pallas_call | solution.py:368
  73.7 174.2 %back.1 = (f32[4,17,24,256]{3,2,1,0:T(8,128)}, bf16[256,1536]{1,0:T(8,128)(2,1)}, bf16[256,1536]{1,0:T(8,128)(2,1)}, f32[8,1536]{1,0:T(8,128)}) custom-call(bf16[1024,2304]{1,0:T(8,128)(2,1)} %get-tuple-element.47.dgu_h, bf16[1024,1152]{1,0:T(8,128)(2,1)} %get-tuple-element.48.a_h, f32[4,2,128,1536]{3,2,1,0:T(8,128)} %get-tuple-element.49.dn2_h, ...), custom_call_target="tpu_custom_call" | custom-call | tf_op jit(solution)/shard_map/back/pallas_call | solution.py:885
  247.9 3.7 %finish.1 = (bf16[256,1536]{1,0:T(8,128)(2,1)}, bf16[256,1536]{1,0:T(8,128)(2,1)}, f32[24]{0:T(128)}, f32[24,768]{1,0:T(8,128)}, f32[6,128]{1,0:T(8,128)}, /*ind...) custom-call(f32[4,17,24,256]{3,2,1,0:T(8,128)} %get-tuple-element.62, ...), custom_call_target="tpu_custom_call" | custom-call | tf_op jit(solution)/shard_map/finish/pallas_call | solution.py:864

commit v5 on v4

--- a/solution.py
+++ b/solution.py
@@ -181,23 +181,26 @@
         qp = dot(n1, wq[:, at]) + bias[h : h + 1]
         q_o[:, at] = (rope(qp, cosine, sine) * WIDTH**-0.5).astype(BF)
 
-    def head(h, _):
-        at = pl.ds(pl.multiple_of(h * WIDTH, WIDTH), WIDTH)
-        s = jnp.where(mask_o[...] > 0.5, dot_nt(q_o[:, at], k_o[...]), NEG_FILL)
-        e = jnp.exp(s - jnp.max(s, axis=-1, keepdims=True))
-        soft = (e / jnp.sum(e, axis=-1, keepdims=True)).astype(BF)
-        o = dot(soft, v_o[...]).astype(BF)
-        o2_o[:TOK, at] = o
-        of[:, at] = o.astype(F32)
-        return 0
-
-    lax.fori_loop(0, HEADS, head, 0)
+    def attend(at_rows):
+        def head(h, _):
+            at = pl.ds(pl.multiple_of(h * WIDTH, WIDTH), WIDTH)
+            s = jnp.where(mask_o[at_rows, :] > 0.5, dot_nt(q_o[at_rows, at], k_o[...]), NEG_FILL)
+            e = jnp.exp(s - jnp.max(s, axis=-1, keepdims=True))
+            soft = (e / jnp.sum(e, axis=-1, keepdims=True)).astype(BF)
+            o = dot(soft, v_o[...]).astype(BF)
+            o2_o[at_rows, at] = o
+            of[at_rows, at] = o.astype(F32)
+            return 0
+
+        lax.fori_loop(0, HEADS, head, 0)
 
     def quarter(n):
         return pl.ds(n * SUB, SUB)
 
+    attend(other)
     part[0] = dot(o2_o[other, :], wo[...])
     halves = [send(part.at[0, quarter(n)], prec.at[quarter(n)], mate) for n in range(2)]
+    attend(mine)
     o_core = send(of, orr, core)
     part[1] = dot(o2_o[mine, :], wo[...])
 
@@ -294,6 +297,9 @@
         early, late = results(n)
         for copy in early:
             copy.start()
+        if n == 3:
+            dy_across.wait_recv()
+            turn(3)
         da = dot_nt(gather(dyf, n), wd[...])
         dg = (da * u * sg * (1.0 + g * (1.0 - sg))).astype(BF)
         du = (da * silu).astype(BF)
@@ -344,8 +350,6 @@
     dy_pass.wait_recv()
     dy_across = send(dyf.at[x2, c], dyf.at[x2, c], core)
     step_two(1)
-    dy_across.wait_recv()
-    turn(3)
     for copy in core_across:
         copy.wait_recv()
     feed(3)

time: 252 us -> 251 us (level)
  no operation moved by 1% of the time
where the time goes in v5:
time: 251 us
  Pallas kernels  250 us (100%)
    pallas_call x1, Pallas kernels, back(): pl.pallas_call(back_kernel, name='back', out_shape=(shape((4, NU, 24, UW)...  174 us
    pallas_call x1, Pallas kernels, front(): pl.pallas_call(front_kernel, name='front', out_shape=(shape((TOK, QW), BF...  72.2 us

profile of v5, /device:TPU:1, one launch (start us, length us, event | category | flops | bytes accessed | tf_op | source)
XLA Modules:
  0.0 250.9 jit_solution(17998579190901308494)
XLA Ops:
  0.6 72.2 %front.1 = (bf16[256,768]{1,0:T(8,128)(2,1)}, bf16[256,128]{1,0:T(8,128)(2,1)}, bf16[256,128]{1,0:T(8,128)(2,1)}, f32[256,256]{1,0:T(8,128)}, f32[256,128]{1,0:T...) custom-call(s32[1,4]{1,0:T(1,128)} %lengths.1, ...), custom_call_target="tpu_custom_call" | custom-call | tf_op jit(solution)/shard_map/front/pallas_call | solution.py:372
  72.8 174.3 %back.1 = (f32[4,17,24,256]{3,2,1,0:T(8,128)}, bf16[256,1536]{1,0:T(8,128)(2,1)}, bf16[256,1536]{1,0:T(8,128)(2,1)}, f32[8,1536]{1,0:T(8,128)}) custom-call(bf16[1024,2304]{1,0:T(8,128)(2,1)} %get-tuple-element.47.dgu_h, bf16[1024,1152]{1,0:T(8,128)(2,1)} %get-tuple-element.48.a_h, f32[4,2,128,1536]{3,2,1,0:T(8,128)} %get-tuple-element.49.dn2_h, ...), custom_call_target="tpu_custom_call" | custom-call | tf_op jit(solution)/shard_map/back/pallas_call | solution.py:889
  247.1 3.7 %finish.1 = (bf16[256,1536]{1,0:T(8,128)(2,1)}, bf16[256,1536]{1,0:T(8,128)(2,1)}, f32[24]{0:T(128)}, f32[24,768]{1,0:T(8,128)}, f32[6,128]{1,0:T(8,128)}, /*ind...) custom-call(f32[4,17,24,256]{3,2,1,0:T(8,128)} %get-tuple-element.62, ...), custom_call_target="tpu_custom_call" | custom-call | tf_op jit(solution)/shard_map/finish/pallas_call | solution.py:868
